TPU v7x, 32 devices: a whole 2x2x4 slice. The times are simulated.
32 devices in a mesh: seq: 8 (over z, y), row: 4 (over x, core).
Axes of the slice: x: 2, y: 2, z: 4, core: 2. Of those that a mesh axis runs over, the one named last changes fastest.
Arguments:
- inputs: float32 [8, 1024, 1024], P('row', 'seq'), may hold values from -6 to 6
- cotangent: float32 [8, 1024, 1024], P('row', 'seq'), may hold values from -6 to 6
- segments: int32 [8, 1024], P('row', 'seq'), may hold values from 0 to 4, as said below
- norm1_gain: bfloat16 [1024], P(('seq', 'row')), may hold values from 0.5 to 1.5
- input_proj: bfloat16 [1024, 1536], P(('seq', 'row')), may hold values from -0.1875 to 0.1875
- branch_proj: bfloat16 [1024, 1536], P(('seq', 'row')), may hold values from -0.1875 to 0.1875
- conv_weight: bfloat16 [4, 1536], P(None, ('seq', 'row')), may hold values from -3 to 3
- conv_bias: bfloat16 [1536], P(('seq', 'row')), may hold values from -2 to 2
- recur_gate: bfloat16 [1536, 128], P(('seq', 'row')), may hold values from -0.5 to 0.5
- input_gate: bfloat16 [1536, 128], P(('seq', 'row')), may hold values from -0.5 to 0.5
- recur_bias: bfloat16 [1536], P(('seq', 'row')), may hold values from -2 to 2
- input_bias: bfloat16 [1536], P(('seq', 'row')), may hold values from -2 to 2
- decay_param: bfloat16 [1536], P(('seq', 'row')), may hold values from -16 to -3
- output_proj: bfloat16 [1536, 1024], P(('seq', 'row')), may hold values from -0.4375 to 0.4375
- norm2_gain: bfloat16 [1024], P(('seq', 'row')), may hold values from 0.5 to 1.5
- mlp_gate: bfloat16 [1024, 3072], P(('seq', 'row')), may hold values from -0.1875 to 0.1875
- mlp_up: bfloat16 [1024, 3072], P(('seq', 'row')), may hold values from -0.1875 to 0.1875
- mlp_down: bfloat16 [3072, 1024], P(('seq', 'row')), may hold values from -0.21875 to 0.21875
Outputs:
- result: float32 [8, 1024, 1024], P('row', 'seq')
- grad_inputs: float32 [8, 1024, 1024], P('row', 'seq')
- grad_norm1_gain: float32 [1024], P(('seq', 'row'))
- grad_input_proj: float32 [1024, 1536], P(('seq', 'row'))
- grad_branch_proj: float32 [1024, 1536], P(('seq', 'row'))
- grad_conv_weight: float32 [4, 1536], P(None, ('seq', 'row'))
- grad_conv_bias: float32 [1536], P(('seq', 'row'))
- grad_recur_gate: float32 [1536, 128], P(('seq', 'row'))
- grad_input_gate: float32 [1536, 128], P(('seq', 'row'))
- grad_recur_bias: float32 [1536], P(('seq', 'row'))
- grad_input_bias: float32 [1536], P(('seq', 'row'))
- grad_decay_param: float32 [1536], P(('seq', 'row'))
- grad_output_proj: float32 [1536, 1024], P(('seq', 'row'))
- grad_norm2_gain: float32 [1024], P(('seq', 'row'))
- grad_mlp_gate: float32 [1024, 3072], P(('seq', 'row'))
- grad_mlp_up: float32 [1024, 3072], P(('seq', 'row'))
- grad_mlp_down: float32 [3072, 1024], P(('seq', 'row'))
Inputs may be any that keep to these rules, and one draw needn't show every extreme that they name: `segments`: within a row the numbers never fall and rise by one at each of four document starts. In even rows two documents start among the first 128 tokens and two among the last 128 tokens. In odd rows one starts among the first 128 tokens, one among the last 128, and the two others lie in the token ranges of the two middle indices of seq, each at least 3 tokens after the range's start.
All inputs are finite; a program needn't handle non-finite values.
Results may differ from a plain program's by a relative error of at most 0.014.
Values may be sent and summed in bfloat16 or wider, within the bound.
No kernel may reach another device: no remote copies, remote signals or barrier semaphores. Data moves between devices by JAX's collectives and lax.ppermute only.
A program may use at most 320 MiB of HBM per device.

v0:
```python
import jax
import jax.numpy as jnp
from jax import lax
from jax.sharding import PartitionSpec as P

EPS = 1e-06


def passed_along(block, axis, distance):
    devices = range(lax.axis_size(axis))
    route = [(i - distance, i) for i in devices if i - distance in devices]
    return lax.ppermute(block, axis, route)


def normed(values, gain):
    return values * lax.rsqrt(jnp.mean(values * values, axis=-1, keepdims=True) + EPS) * gain


def gate_math(recur_pre, input_pre, conv_out, decay_param, reset):
    recur = jax.nn.sigmoid(recur_pre)
    admit = jax.nn.sigmoid(input_pre)
    log_decay = -8.0 * jax.nn.softplus(decay_param) * recur
    decay = jnp.exp(log_decay)
    scaled = jnp.where(reset[..., None], 1.0, jnp.sqrt(-jnp.expm1(2.0 * log_decay)))
    carried = jnp.where(reset[..., None], 0.0, decay)
    return (carried, scaled * admit * conv_out)


def affine(earlier, later):
    return (earlier[0] * later[0], later[0] * earlier[1] + later[1])


def plain_dot(left, right):
    return jnp.dot(left, right, preferred_element_type=jnp.float32)


def left_dot(left, right):
    return lax.dot_general(
        left, right, (((0,), (0,)), ((), ())), preferred_element_type=jnp.float32
    )


def right_dot(left, right):
    return lax.dot_general(
        left, right, (((1,), (1,)), ((), ())), preferred_element_type=jnp.float32
    )


def row_term(left, right):
    return left_dot(left, right)


def block_mix(values, weight):
    block = weight.shape[1]
    heads = weight.shape[0] // block
    shaped = values.reshape(-1, heads, block)
    mixed = jnp.einsum(
        "thi,hio->tho",
        shaped,
        weight.reshape(heads, block, block),
        preferred_element_type=jnp.float32,
    )
    return mixed.reshape(values.shape)


def block_back(grads, weight):
    block = weight.shape[1]
    heads = weight.shape[0] // block
    shaped = grads.reshape(-1, heads, block)
    mixed = jnp.einsum(
        "tho,hio->thi",
        shaped,
        weight.reshape(heads, block, block),
        preferred_element_type=jnp.float32,
    )
    return mixed.reshape(grads.shape)


def block_weight_grad(values, grads, block):
    heads = values.shape[-1] // block
    left_side = values.reshape(-1, heads, block)
    right_side = grads.reshape(-1, heads, block)
    total = jnp.einsum("thi,tho->hio", left_side, right_side, preferred_element_type=jnp.float32)
    return total.reshape(heads * block, block)


def gelu_mul(gate_pre, up_pre):
    return jax.nn.gelu(gate_pre) * up_pre


def on_device(
    inputs,
    cotangent,
    segments,
    norm1_gain,
    input_proj,
    branch_proj,
    conv_weight,
    conv_bias,
    recur_gate,
    input_gate,
    recur_bias,
    input_bias,
    decay_param,
    output_proj,
    norm2_gain,
    mlp_gate,
    mlp_up,
    mlp_down,
):
    (
        gain_one,
        proj_in,
        proj_branch,
        conv_taps,
        conv_shift,
        gate_recur,
        gate_input,
        bias_recur,
        bias_input,
        decay_raw,
        proj_out,
        gain_two,
        gate_mlp,
        up_mlp,
        down_mlp,
    ) = (
        lax.all_gather(norm1_gain, ("seq", "row"), axis=0, tiled=True),
        lax.all_gather(input_proj, ("seq", "row"), axis=0, tiled=True),
        lax.all_gather(branch_proj, ("seq", "row"), axis=0, tiled=True),
        lax.all_gather(conv_weight, ("seq", "row"), axis=1, tiled=True),
        lax.all_gather(conv_bias, ("seq", "row"), axis=0, tiled=True),
        lax.all_gather(recur_gate, ("seq", "row"), axis=0, tiled=True),
        lax.all_gather(input_gate, ("seq", "row"), axis=0, tiled=True),
        lax.all_gather(recur_bias, ("seq", "row"), axis=0, tiled=True),
        lax.all_gather(input_bias, ("seq", "row"), axis=0, tiled=True),
        lax.all_gather(decay_param, ("seq", "row"), axis=0, tiled=True),
        lax.all_gather(output_proj, ("seq", "row"), axis=0, tiled=True),
        lax.all_gather(norm2_gain, ("seq", "row"), axis=0, tiled=True),
        lax.all_gather(mlp_gate, ("seq", "row"), axis=0, tiled=True),
        lax.all_gather(mlp_up, ("seq", "row"), axis=0, tiled=True),
        lax.all_gather(mlp_down, ("seq", "row"), axis=0, tiled=True),
    )
    rows_dev, group, model_width = inputs.shape
    lru_width = proj_in.shape[1]
    ffn_width = gate_mlp.shape[1]
    block_size = gate_recur.shape[1]
    tokens = rows_dev * group
    gain_one = gain_one.astype(jnp.float32)
    gain_two = gain_two.astype(jnp.float32)
    conv_taps = conv_taps.astype(jnp.float32)
    conv_shift = conv_shift.astype(jnp.float32)
    bias_recur = bias_recur.astype(jnp.float32)
    bias_input = bias_input.astype(jnp.float32)
    decay_raw = decay_raw.astype(jnp.float32)
    start = lax.axis_index("seq") * group
    position = start + jnp.arange(group, dtype=jnp.int32)
    prior_ids = passed_along(segments[:, group - 3 :], "seq", 1)
    joined_ids = jnp.concatenate([prior_ids, segments], axis=1)
    masks = []
    for offset in range(4):
        same = (joined_ids[:, 3 - offset : 3 - offset + group] == segments) & (position >= offset)[
            None, :
        ]
        masks.append(same.astype(jnp.float32)[..., None])
    reset = (joined_ids[:, 2 : 2 + group] != segments) | (position == 0)[None, :]
    flat = inputs.reshape(tokens, model_width)
    first = normed(flat, gain_one).astype(jnp.bfloat16)
    mixer_in = plain_dot(first, proj_in).astype(jnp.bfloat16).reshape(rows_dev, group, lru_width)
    branch_pre = plain_dot(first, proj_branch)
    branch = jax.nn.gelu(branch_pre).reshape(rows_dev, group, lru_width)
    prior_rows = passed_along(mixer_in[:, group - 3 :], "seq", 1)
    joined = jnp.concatenate([prior_rows, mixer_in], axis=1).astype(jnp.float32)
    conv_sum = conv_shift
    for offset in range(4):
        conv_sum = (
            conv_sum
            + conv_taps[offset] * joined[:, 3 - offset : 3 - offset + group] * masks[offset]
        )
    conv_low = conv_sum.astype(jnp.bfloat16)
    conv_out = conv_low.astype(jnp.float32)
    recur_pre = block_mix(conv_low, gate_recur) + bias_recur
    input_pre = block_mix(conv_low, gate_input) + bias_input
    carried, driven = gate_math(recur_pre, input_pre, conv_out, decay_raw, reset)
    through, local_state = lax.associative_scan(affine, (carried, driven), axis=1)
    end_map = (through[:, -1], local_state[:, -1])

    def forward_link(counter, carry_value):
        return passed_along(end_map[0] * carry_value + end_map[1], "seq", 1)

    incoming = lax.fori_loop(0, lax.axis_size("seq") - 1, forward_link, jnp.zeros_like(end_map[1]))
    state = local_state + through * incoming[:, None]
    mixed = (state * branch).astype(jnp.bfloat16).reshape(tokens, lru_width)
    middle = flat + plain_dot(mixed, proj_out)
    second = normed(middle, gain_two).astype(jnp.bfloat16)
    gate_pre = plain_dot(second, gate_mlp)
    up_pre = plain_dot(second, up_mlp)
    hidden = gelu_mul(gate_pre, up_pre).astype(jnp.bfloat16)
    result = middle + plain_dot(hidden, down_mlp)
    grad_out = cotangent.reshape(tokens, model_width)
    grad_low = grad_out.astype(jnp.bfloat16)
    grad_hidden = right_dot(grad_low, down_mlp)
    grad_gate_pre, grad_up_pre = jax.vjp(gelu_mul, gate_pre, up_pre)[1](grad_hidden)
    grad_gate_low = grad_gate_pre.astype(jnp.bfloat16)
    grad_up_low = grad_up_pre.astype(jnp.bfloat16)
    grad_second = right_dot(grad_gate_low, gate_mlp) + right_dot(grad_up_low, up_mlp)
    grad_middle_norm, grad_gain_two = jax.vjp(normed, middle, gain_two)[1](grad_second)
    grad_middle = grad_out + grad_middle_norm
    grad_mixed_low = grad_middle.astype(jnp.bfloat16)
    grad_mixed = right_dot(grad_mixed_low, proj_out).reshape(rows_dev, group, lru_width)
    grad_state = grad_mixed * branch
    grad_branch = grad_mixed * state
    next_decay = jnp.concatenate([carried[:, 1:], jnp.ones_like(carried[:, :1])], axis=1)
    reach, local_adjoint = lax.associative_scan(
        affine, (next_decay, grad_state), axis=1, reverse=True
    )
    back_map = (carried[:, 0] * reach[:, 0], carried[:, 0] * local_adjoint[:, 0])

    def backward_link(counter, carry_value):
        return passed_along(back_map[0] * carry_value + back_map[1], "seq", -1)

    outgoing = lax.fori_loop(
        0, lax.axis_size("seq") - 1, backward_link, jnp.zeros_like(back_map[1])
    )
    adjoint = local_adjoint + reach * outgoing[:, None]
    previous = jnp.concatenate([incoming[:, None], state[:, :-1]], axis=1)

    def gate_local(recur_value, input_value, conv_value, decay_value):
        return gate_math(recur_value, input_value, conv_value, decay_value, reset)

    grad_recur_pre, grad_input_pre, grad_conv_direct, grad_decay = jax.vjp(
        gate_local, recur_pre, input_pre, conv_out, decay_raw
    )[1]((adjoint * previous, adjoint))
    recur_low = grad_recur_pre.astype(jnp.bfloat16)
    input_low = grad_input_pre.astype(jnp.bfloat16)
    grad_recur_gate = block_weight_grad(conv_low, recur_low, block_size)
    grad_input_gate = block_weight_grad(conv_low, input_low, block_size)
    grad_recur_bias = jnp.sum(recur_low.astype(jnp.float32), axis=(0, 1))
    grad_input_bias = jnp.sum(input_low.astype(jnp.float32), axis=(0, 1))
    grad_conv = (
        grad_conv_direct + block_back(recur_low, gate_recur) + block_back(input_low, gate_input)
    )
    spread = jnp.zeros((rows_dev, group + 3, lru_width), jnp.float32)
    tap_grads = []
    for offset in range(4):
        masked = grad_conv * masks[offset]
        spread = spread + jnp.pad(
            conv_taps[offset] * masked, ((0, 0), (3 - offset, offset), (0, 0))
        )
        tap_grads.append(jnp.sum(masked * joined[:, 3 - offset : 3 - offset + group], axis=(0, 1)))
    grad_taps = jnp.stack(tap_grads)
    grad_conv_bias = jnp.sum(grad_conv, axis=(0, 1))
    returned = passed_along(spread[:, :3].astype(jnp.bfloat16), "seq", -1).astype(jnp.float32)
    grad_mixer = spread[:, 3:] + jnp.pad(returned, ((0, 0), (group - 3, 0), (0, 0)))
    grad_mixer_low = grad_mixer.astype(jnp.bfloat16).reshape(tokens, lru_width)
    grad_branch_pre = jax.vjp(jax.nn.gelu, branch_pre)[1](grad_branch.reshape(tokens, lru_width))[0]
    grad_branch_low = grad_branch_pre.astype(jnp.bfloat16)
    grad_first = right_dot(grad_mixer_low, proj_in) + right_dot(grad_branch_low, proj_branch)
    grad_flat_norm, grad_gain_one = jax.vjp(normed, flat, gain_one)[1](grad_first)
    grad_inputs = (grad_middle + grad_flat_norm).reshape(inputs.shape)
    paired = jnp.concatenate([grad_gate_low, grad_up_low], axis=1)
    left_sum = lax.psum_scatter(
        row_term(second, paired), ("seq", "row"), scatter_dimension=0, tiled=True
    )
    down_sum = lax.psum_scatter(
        row_term(hidden, grad_low), ("seq", "row"), scatter_dimension=0, tiled=True
    )
    grad_gate = left_sum[:, :ffn_width]
    grad_up = left_sum[:, ffn_width:]
    mixer_pair = jnp.concatenate([grad_mixer_low, grad_branch_low], axis=1)
    left_mixer = lax.psum_scatter(
        row_term(first, mixer_pair), ("seq", "row"), scatter_dimension=0, tiled=True
    )
    grad_proj_out = lax.psum_scatter(
        row_term(mixed, grad_mixed_low), ("seq", "row"), scatter_dimension=0, tiled=True
    )
    small = (
        lax.psum_scatter(grad_gain_one, ("seq", "row"), scatter_dimension=0, tiled=True),
        lax.psum_scatter(grad_taps, ("seq", "row"), scatter_dimension=1, tiled=True),
        lax.psum_scatter(grad_conv_bias, ("seq", "row"), scatter_dimension=0, tiled=True),
        lax.psum_scatter(grad_recur_gate, ("seq", "row"), scatter_dimension=0, tiled=True),
        lax.psum_scatter(grad_input_gate, ("seq", "row"), scatter_dimension=0, tiled=True),
        lax.psum_scatter(grad_recur_bias, ("seq", "row"), scatter_dimension=0, tiled=True),
        lax.psum_scatter(grad_input_bias, ("seq", "row"), scatter_dimension=0, tiled=True),
        lax.psum_scatter(grad_decay, ("seq", "row"), scatter_dimension=0, tiled=True),
        lax.psum_scatter(grad_gain_two, ("seq", "row"), scatter_dimension=0, tiled=True),
    )
    return (
        result.reshape(inputs.shape),
        grad_inputs,
        small[0],
        left_mixer[:, :lru_width],
        left_mixer[:, lru_width:],
        small[1],
        small[2],
        small[3],
        small[4],
        small[5],
        small[6],
        small[7],
        grad_proj_out,
        small[8],
        grad_gate,
        grad_up,
        down_sum,
    )


def solution(mesh):
    in_specs = (
        P("row", "seq", None),
        P("row", "seq", None),
        P("row", "seq"),
        P(("seq", "row")),
        P(("seq", "row"), None),
        P(("seq", "row"), None),
        P(None, ("seq", "row")),
        P(("seq", "row")),
        P(("seq", "row"), None),
        P(("seq", "row"), None),
        P(("seq", "row")),
        P(("seq", "row")),
        P(("seq", "row")),
        P(("seq", "row"), None),
        P(("seq", "row")),
        P(("seq", "row"), None),
        P(("seq", "row"), None),
        P(("seq", "row"), None),
    )
    out_specs = (
        P("row", "seq", None),
        P("row", "seq", None),
        P(("seq", "row")),
        P(("seq", "row"), None),
        P(("seq", "row"), None),
        P(None, ("seq", "row")),
        P(("seq", "row")),
        P(("seq", "row"), None),
        P(("seq", "row"), None),
        P(("seq", "row")),
        P(("seq", "row")),
        P(("seq", "row")),
        P(("seq", "row"), None),
        P(("seq", "row")),
        P(("seq", "row"), None),
        P(("seq", "row"), None),
        P(("seq", "row"), None),
    )
    return jax.shard_map(
        on_device, mesh=mesh, in_specs=in_specs, out_specs=out_specs, check_vma=False
    )
```

profile of v0, /device:TPU:0, one launch (start us, length us, event | category | flops | bytes accessed | tf_op | source)
XLA Modules:
  0.0 1825.0 jit_solution(9556004542207734548)
XLA Ops:
  11.4 4.9 collective-permute-start.2
  21.5 41.1 %all-reduce.76 = (bf16[1536]{0:T(1024)(128)(2,1)S(1)}, bf16[1024]{0:T(1024)(128)(2,1)S(1)}, bf16[1536]{0:T(1024)(128)(2,1)S(1)}, bf16[1536]{0:T(1024)(128)(2,1)S...) all-reduce(bf16[1536]{0:T(1024)(128)(2,1)S(1)} %dynamic-update-slic, ...), channel_id=1, replica_groups=mesh['seq'=8,'row'=4] {'seq','row'}, use_global_device_ids=true, to_apply=%add.63 | all-reduce | flops 8192 | bytes 32768
  64.1 40.6 %all-gather = bf16[32,48,4]{1,2,0:T(4,128)(2,1)S(1)} all-gather(bf16[1,48,4]{1,2,0:T(4,128)(2,1)S(1)} %bitcast.180), channel_id=1, replica_groups=mesh['seq'=8,'row'=4] {'seq','row'}, dimensions={0}, use_global_device_ids=true | all-gather | bytes 12672 | tf_op jit(solution)/shard_map/all_gather | solution.py:131
  104.9 37.9 %all_gather.52 = bf16[1536,128]{1,0:T(8,128)(2,1)S(1)} all-gather(bf16[48,128]{1,0:T(8,128)(2,1)S(1)} %copy-done.106), channel_id=1, replica_groups=mesh['seq'=8,'row'=4] {'seq','row'}, dimensions={0}, use_global_device_ids=true | all-gather | bytes 405504 | tf_op jit(solution)/shard_map/all_gather | solution.py:134
  142.8 42.7 %all_gather.50 = bf16[1536,128]{1,0:T(8,128)(2,1)} all-gather(bf16[48,128]{1,0:T(8,128)(2,1)S(1)} %copy-done.107), channel_id=1, replica_groups=mesh['seq'=8,'row'=4] {'seq','row'}, dimensions={0}, use_global_device_ids=true | all-gather | bytes 405504 | tf_op jit(solution)/shard_map/all_gather | solution.py:133
  191.7 4.6 multiply_multiply_fusion.9
  213.7 5.2 convert_multiply_fusion.1
  300.6 4.4 slice.521
  312.3 4.4 slice.588
  316.8 4.4 slice.597
  412.0 38.1 %while.20 = (s32[]{:T(128)}, f32[2,1536]{1,0:T(2,128)S(1)}, f32[2,1536]{1,0:T(2,128)S(1)}, f32[2,1536]{1,0:T(2,128)S(1)}, s32[]{:T(128)}) while((s32[]{:T(128)}, f32[2,1536]{1,0:T(2,128)S(1)}, f32[2,1536]{1,0:T(2,128)S(1)}, f32[2,1536]{1,0:T(2,128)S(1)}, s32[]{:T(128)}) %tuple.148), condition=%wide.region_2.3_spmd, body=%wide.region_1.2_spmd.sunk | while | flops 6146 | bytes 98405 | solution.py:191
  437.2 5.1 collective-permute-start
  443.7 5.1 collective-permute-start
  450.8 6.9 slice.589
  457.7 6.8 slice.598
  464.5 7.3 slice.591
  471.8 5.6 multiply_convert_fusion.2
  482.9 6.5 fusion.92
  489.4 6.4 fusion.93
  495.8 9.9 multiply_convert_fusion
  505.7 5.8 fusion.94
  529.6 6.9 slice.595
  536.5 6.8 slice.593
  614.1 7.0 slice.643
  706.6 12.8 rev.8
  719.5 12.9 rev.9
  732.4 46.1 %while.21 = (s32[]{:T(128)}, f32[2,1536]{1,0:T(2,128)S(1)}, f32[2,1536]{1,0:T(2,128)S(1)}, f32[2,1536]{1,0:T(2,128)S(1)}, s32[]{:T(128)}) while((s32[]{:T(128)}, f32[2,1536]{1,0:T(2,128)S(1)}, f32[2,1536]{1,0:T(2,128)S(1)}, f32[2,1536]{1,0:T(2,128)S(1)}, s32[]{:T(128)}) %tuple.147), condition=%wide.region_6.7_spmd, body=%wide.region_5.6_spmd.sunk | while | flops 6146 | bytes 98405 | solution.py:222
  733.7 5.5 collective-permute-done.1
  740.5 5.5 collective-permute-done.1
  747.3 5.2 collective-permute-done.1
  753.8 5.2 collective-permute-done.1
  760.3 5.2 collective-permute-done.1
  766.8 5.2 collective-permute-done.1
  773.3 5.2 collective-permute-done.1
  778.6 5.7 multiply_reduce_fusion
  784.3 4.4 convert_reduce_fusion.1
  814.2 4.8 multiply_reduce_fusion.4
  828.2 6.3 fusion.26
  836.2 11.8 fusion.7
  858.2 7.8 fusion.98
  870.3 5.8 convolution_add_fusion.3
  877.3 42.8 %all-reduce.75 = (f32[1024]{0:T(1024)S(1)}, f32[1536]{0:T(1024)S(1)}, f32[1536]{0:T(1024)S(1)}, f32[1536]{0:T(1024)S(1)}, f32[1536]{0:T(1024)S(1)}, /*index=5*/f32[1024]{0:T(1024)S(1)}) all-reduce(f32[1024]{0:T(1024)S(1)} %get-tuple-element.77, f32[1536]{0:T(1024)S(1)} %get-tuple-element.79, ...), channel_id=2, replica_groups=mesh['seq'=8,'row'=4] {'seq','row'}, use_global_device_ids=true, to_apply=%region_9.10.clone | all-reduce | flops 8192 | bytes 65536
  926.3 156.9 %reduce-scatter.10.cloned.1.call-done = f32[32,3072]{1,0:T(8,128)} async-done(((f32[1024,3072]{1,0:T(8,128)}), f32[32,3072]{1,0:T(8,128)}) %reduce-scatter.10.cloned.1.call-update) | async-done | bytes 393232 | tf_op jit(solution)/shard_map/reduce_scatter | solution.py:271
  1085.0 250.3 %reduce-scatter.18.cloned.1.call-done = f32[32,6144]{1,0:T(8,128)} async-done(((f32[1024,6144]{1,0:T(8,128)}), f32[32,6144]{1,0:T(8,128)}) %reduce-scatter.18.cloned.1.call-update) | async-done | bytes 786448 | tf_op jit(solution)/shard_map/reduce_scatter | solution.py:262
  1337.4 98.6 %reduce-scatter.12.cloned.1.call-done = f32[48,128]{1,0:T(8,128)} async-done(((f32[1536,128]{1,0:T(8,128)}), f32[48,128]{1,0:T(8,128)}) %reduce-scatter.12.cloned.1.call-update) | async-done | bytes 24592 | tf_op jit(solution)/shard_map/reduce_scatter | solution.py:281
  1436.0 100.3 %reduce-scatter.14.cloned.1.call-done = f32[48,128]{1,0:T(8,128)} async-done(((f32[1536,128]{1,0:T(8,128)}), f32[48,128]{1,0:T(8,128)}) %reduce-scatter.14.cloned.1.call-update) | async-done | bytes 24592 | tf_op jit(solution)/shard_map/reduce_scatter | solution.py:282
  1536.2 119.5 %reduce-scatter.16.cloned.1.call-done = f32[48,1024]{1,0:T(8,128)} async-done(((f32[1536,1024]{1,0:T(8,128)}), f32[48,1024]{1,0:T(8,128)}) %reduce-scatter.16.cloned.1.call-update) | async-done | bytes 196624 | tf_op jit(solution)/shard_map/reduce_scatter | solution.py:274
  1655.7 162.3 %reduce-scatter.20.cloned.1.call-done = f32[96,1024]{1,0:T(8,128)} async-done(((f32[3072,1024]{1,0:T(8,128)}), f32[96,1024]{1,0:T(8,128)}) %reduce-scatter.20.cloned.1.call-update) | async-done | bytes 393232 | tf_op jit(solution)/shard_map/reduce_scatter | solution.py:265
  (611 shorter events, 492.6 us)
Async XLA Ops:
  7.2 97.7 %copy-start.106 = (bf16[48,128]{1,0:T(8,128)(2,1)S(1)}, bf16[48,128]{1,0:T(8,128)(2,1)}, u32[]{:S(2)}) copy-start(bf16[48,128]{1,0:T(8,128)(2,1)} %param.31) | copy-start | bytes 36868
  7.2 135.6 %copy-start.107 = (bf16[48,128]{1,0:T(8,128)(2,1)S(1)}, bf16[48,128]{1,0:T(8,128)(2,1)}, u32[]{:S(2)}) copy-start(bf16[48,128]{1,0:T(8,128)(2,1)} %param.30) | copy-start | bytes 36868
  7.2 178.9 %copy-start.26 = (f32[2,128,1024]{2,1,0:T(8,128)S(1)}, f32[2,128,1024]{2,1,0:T(8,128)}, u32[]{:S(2)}) copy-start(f32[2,128,1024]{2,1,0:T(8,128)} %param.23) | copy-start | bytes 3145732
  7.2 180.2 %all-gather.8.cloned.1.call-start = ((), (), s32[]{:S(2)}) async-start(), calls=%async_computation.7 | async-start | bytes 3244032 | tf_op jit(solution)/shard_map/all_gather | solution.py:129
  8.0 183.7 %all-gather.10.cloned.1.call-start = ((), (), s32[]{:S(2)}) async-start(), calls=%async_computation.8 | async-start | bytes 3244032 | tf_op jit(solution)/shard_map/all_gather | solution.py:130
  8.7 468.7 %all-gather.12.cloned.1.call-start = ((), (), s32[]{:S(2)}) async-start(), calls=%async_computation.9 | async-start | bytes 3244032 | tf_op jit(solution)/shard_map/all_gather | solution.py:138
  9.4 473.4 %all-gather.14.cloned.1.call-start = ((), (), s32[]{:S(2)}) async-start(), calls=%async_computation.10 | async-start | bytes 6488064 | tf_op jit(solution)/shard_map/all_gather | solution.py:140
  10.0 479.4 %all-gather.16.cloned.1.call-start = ((), (), s32[]{:S(2)}) async-start(), calls=%async_computation.11 | async-start | bytes 6488064 | tf_op jit(solution)/shard_map/all_gather | solution.py:141
  10.6 485.2 %all-gather.18.cloned.1.call-start = ((), (), s32[]{:S(2)}) async-start(), calls=%async_computation.12 | async-start | bytes 6488064 | tf_op jit(solution)/shard_map/all_gather | solution.py:142
  11.4 175.8 %collective-permute-start.2 = (s32[2,3]{1,0:T(2,128)S(1)}, s32[2,3]{1,0:T(2,128)S(1)}, u32[]{:S(2)}, u32[]{:S(2)}) collective-permute-start(s32[2,3]{1,0:T(2,128)S(1)} %slice.507), channel_id=1, source_target_pairs={{0,4},{4,8},{8,12},{12,16},{16,20},{20,24},{24,28},{1,5},{5,9},{9,... | collective-permute-start | bytes 80 | tf_op jit(solution)/shard_map/ppermute | solution.py:12
  16.3 908.6 %reduce-scatter.22.cloned.1.call-start = ((), (), s32[]{:S(2)}) async-start(), calls=%async_computation.19 | async-start | bytes 811008
  16.4 197.3 %copy-start.98 = (f32[128]{0:T(128)}, f32[128]{0:T(128)S(1)}, u32[]{:S(2)}) copy-start(f32[128]{0:T(128)S(1)} %compare_convert_fusion) | copy-start | bytes 1540
  62.6 124.5 %copy-start.73 = (f32[1024]{0:T(1024)}, f32[1024]{0:T(1024)S(1)}, u32[]{:S(2)}) copy-start(f32[1024]{0:T(1024)S(1)} %convert_element_type.103) | copy-start | bytes 12292
  64.0 123.2 %copy-start.108 = (f32[2,128]{1,0:T(2,128)}, f32[2,128]{1,0:T(2,128)S(1)}, u32[]{:S(2)}) copy-start(f32[2,128]{1,0:T(2,128)S(1)} %multiply_reduce_fusion.9) | copy-start | bytes 3076
  64.0 123.1 %copy-start.1 = (f32[2,128,1024]{2,1,0:T(8,128)S(1)}, f32[2,128,1024]{2,1,0:T(8,128)}, u32[]{:S(2)}) copy-start(f32[2,128,1024]{2,1,0:T(8,128)} %param.22) | copy-start | bytes 3145732
  64.0 123.2 %copy-start.102 = (f32[256]{0:T(256)}, f32[256]{0:T(256)S(1)}, u32[]{:S(2)}) copy-start(f32[256]{0:T(256)S(1)} %bitcast_rsqrt_fusion) | copy-start | bytes 3076
  64.0 149.6 %copy-start.58 = (f32[1536]{0:T(1024)}, f32[1536]{0:T(1024)S(1)}, u32[]{:S(2)}) copy-start(f32[1536]{0:T(1024)S(1)} %fusion.67) | copy-start | bytes 18436
  104.8 108.8 %copy-start.54 = (f32[1536]{0:T(1024)}, f32[1536]{0:T(1024)S(1)}, u32[]{:S(2)}) copy-start(f32[1536]{0:T(1024)S(1)} %get-tuple-element.82) | copy-start | bytes 18436
  104.8 108.8 %copy-start.56 = (f32[1536]{0:T(1024)}, f32[1536]{0:T(1024)S(1)}, u32[]{:S(2)}) copy-start(f32[1536]{0:T(1024)S(1)} %get-tuple-element.83) | copy-start | bytes 18436
  104.9 108.8 %copy-start.64 = (f32[1536]{0:T(1024)}, f32[1536]{0:T(1024)S(1)}, u32[]{:S(2)}) copy-start(f32[1536]{0:T(1024)S(1)} %convert_element_type.101) | copy-start | bytes 18436
  142.8 59.4 %copy-start.32 = (bf16[1536,128]{1,0:T(8,128)(2,1)}, bf16[1536,128]{1,0:T(8,128)(2,1)S(1)}, u32[]{:S(2)}) copy-start(bf16[1536,128]{1,0:T(8,128)(2,1)S(1)} %all_gather.52) | copy-start | bytes 1179652
  142.8 70.9 %copy-start.60 = (f32[1536]{0:T(1024)}, f32[1536]{0:T(1024)S(1)}, u32[]{:S(2)}) copy-start(f32[1536]{0:T(1024)S(1)} %convert_element_type.113) | copy-start | bytes 18436
  190.4 6.0 collective-permute-start.3
  412.1 2.7 collective-permute-start
  414.8 5.6 collective-permute-start
  420.4 5.6 collective-permute-start
  426.0 5.6 collective-permute-start
  431.6 5.6 collective-permute-start
  437.2 6.5 collective-permute-start
  443.7 6.5 collective-permute-start
  719.4 59.1 %copy-start.63 = (f32[1536]{0:T(1024)S(1)}, f32[1536]{0:T(1024)}, u32[]{:S(2)}) copy-start(f32[1536]{0:T(1024)} %copy-done.62) | copy-start | bytes 18436
  719.4 59.1 %copy-start.65 = (f32[1536]{0:T(1024)S(1)}, f32[1536]{0:T(1024)}, u32[]{:S(2)}) copy-start(f32[1536]{0:T(1024)} %copy-done.64) | copy-start | bytes 18436
  719.5 59.1 %copy-start.76 = (f32[2,128]{1,0:T(2,128)S(1)}, f32[2,128]{1,0:T(2,128)}, u32[]{:S(2)}) copy-start(f32[2,128]{1,0:T(2,128)} %copy-done.75) | copy-start | bytes 3076
  719.5 59.1 %copy-start.78 = (f32[2,128]{1,0:T(2,128)S(1)}, f32[2,128]{1,0:T(2,128)}, u32[]{:S(2)}) copy-start(f32[2,128]{1,0:T(2,128)} %copy-done.77) | copy-start | bytes 3076
  732.4 6.8 collective-permute-start.1
  739.2 6.8 collective-permute-start.1
  746.0 6.5 collective-permute-start.1
  752.5 6.5 collective-permute-start.1
  759.0 6.5 collective-permute-start.1
  765.5 6.5 collective-permute-start.1
  772.0 6.5 collective-permute-start.1
  820.4 6.7 collective-permute-start.4
  823.2 260.1 %reduce-scatter.10.cloned.1.call-start = ((), (), s32[]{:S(2)}) async-start(), calls=%async_computation.13 | async-start | bytes 12976128 | tf_op jit(solution)/shard_map/reduce_scatter | solution.py:271
  834.6 500.7 %reduce-scatter.18.cloned.1.call-start = ((), (), s32[]{:S(2)}) async-start(), calls=%async_computation.17 | async-start | bytes 25952256 | tf_op jit(solution)/shard_map/reduce_scatter | solution.py:262
  848.0 588.0 %reduce-scatter.12.cloned.1.call-start = ((), (), s32[]{:S(2)}) async-start(), calls=%async_computation.14 | async-start | bytes 811008 | tf_op jit(solution)/shard_map/reduce_scatter | solution.py:281
  850.7 685.5 %reduce-scatter.14.cloned.1.call-start = ((), (), s32[]{:S(2)}) async-start(), calls=%async_computation.15 | async-start | bytes 811008 | tf_op jit(solution)/shard_map/reduce_scatter | solution.py:282
  853.4 802.4 %reduce-scatter.16.cloned.1.call-start = ((), (), s32[]{:S(2)}) async-start(), calls=%async_computation.16 | async-start | bytes 6488064 | tf_op jit(solution)/shard_map/reduce_scatter | solution.py:274
  857.2 960.8 %reduce-scatter.20.cloned.1.call-start = ((), (), s32[]{:S(2)}) async-start(), calls=%async_computation.18 | async-start | bytes 12976128 | tf_op jit(solution)/shard_map/reduce_scatter | solution.py:265
  (96 other events, 1141.4 us)
Sparse Core Ops, SparseCore 0:
  10.9 61.9 all-gather.7
  75.8 58.4 all-gather.9
  137.1 59.1 all-gather.11
  199.0 68.3 all-gather.13
  270.1 68.0 all-gather.15
  340.9 68.0 all-gather.17
  823.3 99.3 reduce-scatter.21
  928.7 154.4 reduce-scatter.9
  1090.8 244.4 reduce-scatter.17
  1340.9 95.0 reduce-scatter.11
  1441.7 94.5 reduce-scatter.13
  1542.3 113.3 reduce-scatter.15
  1663.4 154.5 reduce-scatter.19
where the time goes:
time: 1840 us; the launch traced here: 1820 us
  waiting for transfers between devices  939 us (51%)
  local copies, waits for them, and re-layouts  384 us (21%)
  blocking collectives  205 us (11%)
  other arithmetic  142 us (8%)
  matrix products  92.7 us (5%)
  starting transfers between devices  45.7 us (2%)
    reduce_scatter x1, waiting for transfers between devices, on_device(): lax.psum_scatter(row_term(second, paired), ('seq', 'row'), scatter_dimens...  250 us
    reduce_scatter x1, waiting for transfers between devices, on_device(): lax.psum_scatter(row_term(hidden, grad_low), ('seq', 'row'), scatter_dime...  162 us
    reduce_scatter x1, waiting for transfers between devices, on_device(): lax.psum_scatter(row_term(first, mixer_pair), ('seq', 'row'), scatter_dim...  157 us
    slice x49, local copies, waits for them, and re-layouts, on_device(): lax.associative_scan(affine, (next_decay, grad_state), axis=1, reverse=True)  120 us
    reduce_scatter x1, waiting for transfers between devices, on_device(): lax.psum_scatter(row_term(mixed, grad_mixed_low), ('seq', 'row'), scatter...  119 us
    reduce_scatter x1, waiting for transfers between devices, on_device(): lax.psum_scatter(grad_input_gate, ('seq', 'row'), scatter_dimension=0, ti...  100 us
    reduce_scatter x1, waiting for transfers between devices, on_device(): lax.psum_scatter(grad_recur_gate, ('seq', 'row'), scatter_dimension=0, ti...  98.6 us
    unnamed x2, blocking collectives  83.9 us
  transfers between devices with their start and end apart: 30, of which 21 were waited for; matrix products, arithmetic and copies ran while one was open for 18% of the time, Pallas kernels for 0%

commit v1 on v0

v1 whole, which is shorter than its diff:
```python
import functools
import math

import jax
import jax.numpy as jnp
from jax import lax
from jax.experimental import pallas as pl
from jax.experimental.pallas import tpu as pltpu
from jax.sharding import PartitionSpec as P

EPS = 1e-06
BF = jnp.bfloat16
F32 = jnp.float32
AXES = ("seq", "row")
MIB = 1 << 20
TILE = 256
HALO = 8
GELU_C = math.sqrt(2.0 / math.pi)


class Place:
    def __init__(self):
        seq, row = lax.axis_size("seq"), lax.axis_size("row")
        ny = 1 << ((seq.bit_length() - 1) // 2)
        self.size = {"z": seq // ny, "y": ny, "x": row // 2, "c": 2}
        self.seq, self.row = seq, row
        s, r = lax.axis_index("seq"), lax.axis_index("row")
        self.s = s
        self.at = {"z": s // ny, "y": s % ny, "x": r // 2, "c": r % 2}
        self.stride = {"z": ny * row, "y": row, "x": 2, "c": 1}
        self.chips = seq * (row // 2)

    def swap(self, value, axis, distance):
        pairs = []
        for i in range(self.seq * self.row):
            place = (i // self.stride[axis]) % self.size[axis]
            pairs.append((i, i + ((place ^ distance) - place) * self.stride[axis]))
        return lax.ppermute(value, AXES, pairs)

    def along(self, value, distance):
        pairs = []
        for s in range(self.seq):
            if 0 <= s + distance < self.seq:
                for r in range(self.row):
                    pairs.append((s * self.row + r, (s + distance) * self.row + r))
        return lax.ppermute(value, AXES, pairs)

    def ordered(self, axis, bit, mine, other):
        high = (self.at[axis] & bit) != 0
        return jnp.where(high, other, mine), jnp.where(high, mine, other)

    def gather(self, value, axis, dim):
        distance = 1
        while distance < self.size[axis]:
            other = self.swap(value, axis, distance)
            value = jnp.concatenate(self.ordered(axis, distance, value, other), axis=dim)
            distance *= 2
        return value

    def scatter(self, value, axis, dim, dtype=BF, between=BF):
        distance = self.size[axis] // 2
        while distance:
            half = value.shape[dim] // 2
            high = (self.at[axis] // distance) % 2
            send = lax.dynamic_slice_in_dim(value, (1 - high) * half, half, dim)
            keep = lax.dynamic_slice_in_dim(value, high * half, half, dim)
            other = self.swap(send, axis, distance)
            distance //= 2
            value = (keep.astype(F32) + other.astype(F32)).astype(between if distance else dtype)
        return value


def gather_group(place, value, cut):
    value = place.gather(value[None, None, None], "z", 0)
    left, right = value[..., :cut], value[..., cut:]
    left = place.gather(left, "y", 1)
    right = place.gather(right, "x", 2)
    left = place.gather(left, "x", 2)
    right = place.gather(right, "y", 1)
    return left, right


def scatter_group(place, left, right, last=F32):
    lead = (place.size["z"], place.size["y"], place.size["x"])
    left = left.reshape(lead + left.shape[-2:])
    right = right.reshape(lead + right.shape[-2:])
    left = place.scatter(left, "x", 2)
    right = place.scatter(right, "y", 1)
    left = place.scatter(left, "y", 1)
    right = place.scatter(right, "x", 2)
    both = jnp.concatenate([left, right], axis=-1)
    return place.scatter(both, "z", 0, last)[0, 0, 0]


def compose(earlier, later):
    return jnp.concatenate(
        [earlier[:4] * later[:4], later[:4] * earlier[4:] + later[4:]], axis=0
    )


def carry_in(place, end_map, sign):
    n = place.seq
    unit = jnp.concatenate([jnp.ones_like(end_map[:4]), jnp.zeros_like(end_map[4:])], axis=0)

    def fetched(value, distance):
        got = place.along(value, sign * distance)
        inside = (place.s >= distance) if sign > 0 else (place.s < n - distance)
        return jnp.where(inside, got, unit)

    window, width, first = end_map, 1, True
    total = None
    reach = 0
    while reach < n - 1:
        if first:
            parts = [fetched(window, d) for d in range(1, min(4, n))]
            total = parts[0]
            for part in parts[1:]:
                total = compose(part, total)
            reach = len(parts)
            first = False
        else:
            shifts = []
            d = reach
            while d < n - 1 and len(shifts) < 3:
                shifts.append(d)
                d += reach
            parts = [fetched(total, d) for d in shifts]
            for part in parts:
                total = compose(part, total)
            reach = reach * (len(shifts) + 1)
    return total[4:]


def dot(a, b):
    return jnp.dot(a, b, preferred_element_type=F32)


def dot_nt(a, b):
    return lax.dot_general(a, b, (((1,), (1,)), ((), ())), preferred_element_type=F32)


def dot_tn(a, b):
    return lax.dot_general(a, b, (((0,), (0,)), ((), ())), preferred_element_type=F32)


def moved(value, distance, fill):
    n = value.shape[0]
    size = abs(distance)
    edge = jnp.full((size,) + value.shape[1:], fill, value.dtype)
    if size % 8 == 0:
        if distance > 0:
            return jnp.concatenate([edge, value[: n - size]], axis=0)
        return jnp.concatenate([value[size:], edge], axis=0)
    at = lax.broadcasted_iota(jnp.int32, value.shape, 0)
    turned = pltpu.roll(value, distance % n, 0)
    inside = at >= size if distance > 0 else at < n - size
    return jnp.where(inside, turned, fill)


def scan_tile(decay, drive, sign):
    n = decay.shape[0]
    distance = 1
    while distance < n:
        drive = decay * moved(drive, sign * distance, 0.0) + drive
        decay = decay * moved(decay, sign * distance, 1.0)
        distance *= 2
    return decay, drive


def one_less_exp(u):
    term = jnp.full_like(u, 1.0 / 3628800.0)
    for k in (362880, 40320, 5040, 720, 120, 24, 6, 2):
        term = 1.0 / k - u * term
    small = u * (1.0 - u * term)
    return jnp.where(u < 0.8, small, 1.0 - jnp.exp(-u))


def gelu_parts(value):
    square = value * value
    t = jnp.tanh(GELU_C * value * (1.0 + 0.044715 * square))
    half = 0.5 * (1.0 + t)
    slope = half + 0.5 * value * (1.0 - t * t) * GELU_C * (1.0 + 3.0 * 0.044715 * square)
    return value * half, slope


def full(shape):
    return pl.BlockSpec(shape, lambda j: (0,) * len(shape))


def columns(rows, width=TILE):
    return pl.BlockSpec((rows, width), lambda j: (0, j))


def lines(rows, width):
    return pl.BlockSpec((rows, width), lambda j: (j, 0))


def shape_of(shape, dtype):
    return jax.ShapeDtypeStruct(shape, dtype)


def params(limit):
    return pltpu.CompilerParams(vmem_limit_bytes=limit * MIB)


def forward_kernel(
    n_rows,
    group,
    block,
    first_ref,
    w_ref,
    vec_ref,
    mask_ref,
    gr_ref,
    gi_ref,
    mixer_ref,
    conv_ref,
    rpre_ref,
    ipre_ref,
    through_ref,
    local_ref,
    ends_ref,
    ext_ref,
):
    mixer = dot(first_ref[...], w_ref[...]).astype(BF)
    mixer_ref[...] = mixer
    wide = mixer.astype(F32)
    tokens = n_rows * group
    for r in range(n_rows):
        ext_ref[r, 0:HALO] = wide[tokens + HALO * r : tokens + HALO * (r + 1)]
        ext_ref[r, HALO : HALO + group] = wide[r * group : (r + 1) * group]
    for r in range(n_rows):
        span = slice(r * group, (r + 1) * group)
        conv = vec_ref[4:5] + vec_ref[0:1] * ext_ref[r, HALO : HALO + group]
        for k in range(1, 4):
            conv += (
                vec_ref[k : k + 1]
                * ext_ref[r, HALO - k : HALO - k + group]
                * mask_ref[span, k : k + 1]
            )
        conv_ref[span] = conv.astype(BF)
    for h in range(w_ref.shape[1] // block):
        cols = slice(h * block, (h + 1) * block)
        low = conv_ref[:, cols]
        rpre_ref[:, cols] = dot(low, gr_ref[cols]) + vec_ref[5:6, cols]
        ipre_ref[:, cols] = dot(low, gi_ref[cols]) + vec_ref[6:7, cols]
        for r in range(n_rows):
            span = slice(r * group, (r + 1) * group)
            recur = jax.nn.sigmoid(rpre_ref[span, cols])
            admit = jax.nn.sigmoid(ipre_ref[span, cols])
            rate = vec_ref[7:8, cols] * recur
            reset = mask_ref[span, 0:1]
            decay = jnp.exp(-rate) * (1.0 - reset)
            scale = jnp.where(reset > 0.5, 1.0, jnp.sqrt(one_less_exp(2.0 * rate)))
            drive = scale * admit * conv_ref[span, cols].astype(F32)
            decay, drive = scan_tile(decay, drive, 1)
            through_ref[span, cols] = decay
            local_ref[span, cols] = drive
            ends_ref[r : r + 1, cols] = decay[group - 1 : group]
            ends_ref[n_rows + r : n_rows + r + 1, cols] = drive[group - 1 : group]


def forward_call(first, w_in, vec, masks, gate_r, gate_i, n_rows, group):
    length, model = first.shape
    width, block = w_in.shape[1], gate_r.shape[1]
    tokens = n_rows * group
    tile = TILE
    return pl.pallas_call(
        functools.partial(forward_kernel, n_rows, group, block),
        grid=(width // tile,),
        in_specs=[
            full((length, model)),
            columns(model),
            columns(8),
            full(masks.shape),
            lines(tile, block),
            lines(tile, block),
        ],
        out_specs=[columns(length)] + [columns(tokens)] * 5 + [columns(2 * n_rows)],
        out_shape=[
            shape_of((length, width), BF),
            shape_of((tokens, width), BF),
            shape_of((tokens, width), F32),
            shape_of((tokens, width), F32),
            shape_of((tokens, width), F32),
            shape_of((tokens, width), F32),
            shape_of((2 * n_rows, width), F32),
        ],
        scratch_shapes=[pltpu.VMEM((n_rows, HALO + group, tile), F32)],
        compiler_params=params(24),
        name="recurrence_forward",
    )(first, w_in, vec, masks, gate_r, gate_i)


def mix_kernel(
    n_rows, group, local_ref, through_ref, enter_ref, bpre_ref, w_ref, state_ref, mixed_ref, part_ref
):
    for r in range(n_rows):
        span = slice(r * group, (r + 1) * group)
        state = local_ref[span] + through_ref[span] * enter_ref[r : r + 1]
        state_ref[span] = state
        branch, _ = gelu_parts(bpre_ref[span])
        mixed_ref[span] = (state * branch).astype(BF)
    part = dot(mixed_ref[...], w_ref[...])

    @pl.when(pl.program_id(0) == 0)
    def _():
        part_ref[...] = part

    @pl.when(pl.program_id(0) > 0)
    def _():
        part_ref[...] += part


def mix_call(local, through, enter, branch_pre, w_out, n_rows, group):
    tokens, width = local.shape
    model = w_out.shape[1]
    return pl.pallas_call(
        functools.partial(mix_kernel, n_rows, group),
        grid=(width // TILE,),
        in_specs=[
            columns(tokens),
            columns(tokens),
            columns(n_rows),
            columns(tokens),
            lines(TILE, model),
        ],
        out_specs=[columns(tokens), columns(tokens), full((tokens, model))],
        out_shape=[
            shape_of((tokens, width), F32),
            shape_of((tokens, width), BF),
            shape_of((tokens, model), F32),
        ],
        compiler_params=params(24),
        name="mix",
    )(local, through, enter, branch_pre, w_out)


def ffn_kernel(
    second_ref, low_ref, wg_ref, wu_ref, wd_ref, gg_ref, gu_ref, gd_ref, part_ref, back_ref, turned_ref
):
    step = pl.program_id(0)

    @pl.when(step == 0)
    def _():
        turned_ref[...] = second_ref[...].T

    second, low = second_ref[...], low_ref[...]
    gate = dot(second, wg_ref[...])
    up = dot(second, wu_ref[...])
    grad = dot_nt(low, wd_ref[...])
    active, slope = gelu_parts(gate)
    hidden = (active * up).astype(BF)
    gate_low = (grad * up * slope).astype(BF)
    up_low = (grad * active).astype(BF)
    gg_ref[...] = dot(turned_ref[...], gate_low).astype(BF)
    gu_ref[...] = dot(turned_ref[...], up_low).astype(BF)
    gd_ref[...] = dot_tn(hidden, low).astype(BF)
    part = dot(hidden, wd_ref[...])
    back = dot_nt(gate_low, wg_ref[...]) + dot_nt(up_low, wu_ref[...])

    @pl.when(step == 0)
    def _():
        part_ref[...] = part
        back_ref[...] = back

    @pl.when(step > 0)
    def _():
        part_ref[...] += part
        back_ref[...] += back


def ffn_call(second, low, w_gate, w_up, w_down):
    tokens, model = second.shape
    width = w_gate.shape[1]
    return pl.pallas_call(
        ffn_kernel,
        grid=(width // TILE,),
        in_specs=[
            full((tokens, model)),
            full((tokens, model)),
            columns(model),
            columns(model),
            lines(TILE, model),
        ],
        out_specs=[
            columns(model),
            columns(model),
            lines(TILE, model),
            full((tokens, model)),
            full((tokens, model)),
        ],
        out_shape=[
            shape_of((model, width), BF),
            shape_of((model, width), BF),
            shape_of((width, model), BF),
            shape_of((tokens, model), F32),
            shape_of((tokens, model), F32),
        ],
        scratch_shapes=[pltpu.VMEM((model, tokens), BF)],
        compiler_params=params(40),
        name="feed_forward",
    )(second, low, w_gate, w_up, w_down)


def decay_of(rpre, vec7, reset):
    recur = jax.nn.sigmoid(rpre)
    rate = vec7 * recur
    return recur, rate, jnp.exp(-rate) * (1.0 - reset)


def back_kernel(
    n_rows,
    group,
    low_ref,
    w_ref,
    bpre_ref,
    state_ref,
    rpre_ref,
    mixed_ref,
    vec_ref,
    mask_ref,
    first_ref,
    go_ref,
    gb_ref,
    gbl_ref,
    reach_ref,
    local_ref,
    ends_ref,
    turned_ref,
    grad_ref,
):
    @pl.when(pl.program_id(0) == 0)
    def _():
        turned_ref[...] = first_ref[...].T

    low = low_ref[...]
    grad_ref[...] = dot_nt(low, w_ref[...])
    go_ref[...] = dot_tn(mixed_ref[...], low).astype(BF)
    half = w_ref.shape[0] // 2
    for h in range(2):
        cols = slice(h * half, (h + 1) * half)
        for r in range(n_rows):
            span = slice(r * group, (r + 1) * group)
            branch, slope = gelu_parts(bpre_ref[span, cols])
            grad = grad_ref[span, cols]
            gbl_ref[span, cols] = (grad * state_ref[span, cols] * slope).astype(BF)
            _, _, decay = decay_of(rpre_ref[span, cols], vec_ref[7:8, cols], mask_ref[span, 0:1])
            ahead = moved(decay, -1, 1.0)
            reach, local = scan_tile(ahead, grad * branch, -1)
            reach_ref[span, cols] = reach
            local_ref[span, cols] = local
            ends_ref[r : r + 1, cols] = decay[0:1] * reach[0:1]
            ends_ref[n_rows + r : n_rows + r + 1, cols] = decay[0:1] * local[0:1]
    gb_ref[...] = dot(turned_ref[...], gbl_ref[...]).astype(BF)


def back_call(low, w_out, branch_pre, state, rpre, mixed, vec, masks, first, n_rows, group):
    tokens, model = low.shape
    width = w_out.shape[0]
    return pl.pallas_call(
        functools.partial(back_kernel, n_rows, group),
        grid=(width // TILE,),
        in_specs=[
            full((tokens, model)),
            lines(TILE, model),
            columns(tokens),
            columns(tokens),
            columns(tokens),
            columns(tokens),
            columns(8),
            full(masks.shape),
            full((tokens, model)),
        ],
        out_specs=[
            lines(TILE, model),
            columns(model),
            columns(tokens),
            columns(tokens),
            columns(tokens),
            columns(2 * n_rows),
        ],
        out_shape=[
            shape_of((width, model), BF),
            shape_of((model, width), BF),
            shape_of((tokens, width), BF),
            shape_of((tokens, width), F32),
            shape_of((tokens, width), F32),
            shape_of((2 * n_rows, width), F32),
        ],
        scratch_shapes=[pltpu.VMEM((model, tokens), BF), pltpu.VMEM((tokens, TILE), F32)],
        compiler_params=params(32),
        name="recurrence_back",
    )(low, w_out, branch_pre, state, rpre, mixed, vec, masks, first)


def gates_kernel(
    n_rows,
    group,
    block,
    reach_ref,
    local_ref,
    leave_ref,
    state_ref,
    enter_ref,
    rpre_ref,
    ipre_ref,
    conv_ref,
    mixer_ref,
    vec_ref,
    mask_ref,
    gr_ref,
    gi_ref,
    first_ref,
    win_ref,
    wbr_ref,
    gbl_ref,
    gin_ref,
    ggr_ref,
    ggi_ref,
    gvec_ref,
    gfirst_ref,
    turned_ref,
    rlow_ref,
    ilow_ref,
    gconv_ref,
    ext_ref,
    spread_ref,
    gm_ref,
):
    step = pl.program_id(0)
    tokens = n_rows * group

    @pl.when(step == 0)
    def _():
        turned_ref[...] = first_ref[...].T

    gvec_ref[...] = jnp.zeros_like(gvec_ref)
    for h in range(win_ref.shape[1] // block):
        cols = slice(h * block, (h + 1) * block)
        for r in range(n_rows):
            span = slice(r * group, (r + 1) * group)
            adjoint = local_ref[span, cols] + reach_ref[span, cols] * leave_ref[r : r + 1, cols]
            state = state_ref[span, cols]
            at = lax.broadcasted_iota(jnp.int32, state.shape, 0)
            before = jnp.where(at == 0, enter_ref[r : r + 1, cols], pltpu.roll(state, 1, 0))
            reset = mask_ref[span, 0:1]
            live = 1.0 - reset
            recur, rate, decay = decay_of(rpre_ref[span, cols], vec_ref[7:8, cols], reset)
            admit = jax.nn.sigmoid(ipre_ref[span, cols])
            full_decay = jnp.exp(-rate)
            root = jnp.sqrt(one_less_exp(2.0 * rate))
            scale = jnp.where(reset > 0.5, 1.0, root)
            conv = conv_ref[span, cols].astype(F32)
            direct = adjoint * scale
            gadmit = direct * conv
            gconv_ref[span, cols] = direct * admit
            gscale = adjoint * admit * conv
            glog = live * full_decay * (adjoint * before - gscale * full_decay / root)
            gvec_ref[7:8, cols] += jnp.sum(glog * recur, axis=0, keepdims=True)
            grecur = -(vec_ref[7:8, cols] * glog) * recur * (1.0 - recur)
            ginput = gadmit * admit * (1.0 - admit)
            rlow, ilow = grecur.astype(BF), ginput.astype(BF)
            rlow_ref[span, cols] = rlow
            ilow_ref[span, cols] = ilow
            gvec_ref[5:6, cols] += jnp.sum(rlow.astype(F32), axis=0, keepdims=True)
            gvec_ref[6:7, cols] += jnp.sum(ilow.astype(F32), axis=0, keepdims=True)
        rlow, ilow = rlow_ref[:, cols], ilow_ref[:, cols]
        low = conv_ref[:, cols]
        ggr_ref[cols] = dot_tn(low, rlow)
        ggi_ref[cols] = dot_tn(low, ilow)
        gconv_ref[:, cols] += dot_nt(rlow, gr_ref[cols]) + dot_nt(ilow, gi_ref[cols])
        for r in range(n_rows):
            span = slice(r * group, (r + 1) * group)
            head = slice(tokens + HALO * r, tokens + HALO * (r + 1))
            ext_ref[0:HALO] = mixer_ref[head, cols].astype(F32)
            ext_ref[HALO : HALO + group] = mixer_ref[span, cols].astype(F32)
            gconv = gconv_ref[span, cols]
            gvec_ref[4:5, cols] += jnp.sum(gconv, axis=0, keepdims=True)
            gvec_ref[0:1, cols] += jnp.sum(
                gconv * ext_ref[HALO : HALO + group], axis=0, keepdims=True
            )
            spread_ref[0:HALO] = jnp.zeros((HALO, block), F32)
            spread_ref[HALO : HALO + group] = vec_ref[0:1, cols] * gconv
            for k in range(1, 4):
                masked = gconv * mask_ref[span, k : k + 1]
                there = slice(HALO - k, HALO - k + group)
                gvec_ref[k : k + 1, cols] += jnp.sum(
                    masked * ext_ref[there], axis=0, keepdims=True
                )
                spread_ref[there] += vec_ref[k : k + 1, cols] * masked
            gm_ref[head, cols] = spread_ref[0:HALO].astype(BF)
            gm_ref[span, cols] = spread_ref[HALO : HALO + group].astype(BF)
    gm = gm_ref[...]
    gin_ref[...] = dot(turned_ref[...], gm).astype(BF)
    part = dot_nt(gm, win_ref[...])
    part_branch = dot_nt(gbl_ref[...], wbr_ref[...])

    @pl.when(step == 0)
    def _():
        gfirst_ref[...] = part

    @pl.when(step > 0)
    def _():
        gfirst_ref[...] += part

    gfirst_ref[0:tokens] += part_branch


def gates_call(
    reach, local, leave, state, enter, rpre, ipre, conv, mixer, vec, masks, gate_r, gate_i, first, w_in, w_branch, gbl, n_rows, group
):
    length, model = first.shape
    tokens, width = state.shape
    block = gate_r.shape[1]
    tile = TILE
    return pl.pallas_call(
        functools.partial(gates_kernel, n_rows, group, block),
        grid=(width // tile,),
        in_specs=[
            columns(tokens),
            columns(tokens),
            columns(n_rows),
            columns(tokens),
            columns(n_rows),
            columns(tokens),
            columns(tokens),
            columns(tokens),
            columns(length),
            columns(8),
            full(masks.shape),
            lines(tile, block),
            lines(tile, block),
            full((length, model)),
            columns(model),
            columns(model),
            columns(tokens),
        ],
        out_specs=[
            columns(model),
            lines(tile, block),
            lines(tile, block),
            columns(8),
            full((length, model)),
        ],
        out_shape=[
            shape_of((model, width), BF),
            shape_of((width, block), F32),
            shape_of((width, block), F32),
            shape_of((8, width), F32),
            shape_of((length, model), F32),
        ],
        scratch_shapes=[
            pltpu.VMEM((model, length), BF),
            pltpu.VMEM((tokens, tile), BF),
            pltpu.VMEM((tokens, tile), BF),
            pltpu.VMEM((tokens, tile), F32),
            pltpu.VMEM((HALO + group, block), F32),
            pltpu.VMEM((HALO + group, block), F32),
            pltpu.VMEM((length, tile), BF),
        ],
        compiler_params=params(40),
        name="recurrence_gates",
    )(reach, local, leave, state, enter, rpre, ipre, conv, mixer, vec, masks, gate_r, gate_i, first, w_in, w_branch, gbl)


def normed(values, gain):
    return values * lax.rsqrt(jnp.mean(values * values, axis=-1, keepdims=True) + EPS) * gain


def halves(value, place, dim):
    half = value.shape[dim] // 2
    mine = lax.dynamic_slice_in_dim(value, place.at["c"] * half, half, dim)
    other = lax.dynamic_slice_in_dim(value, (1 - place.at["c"]) * half, half, dim)
    return mine, other


def own_channels(place, value):
    mine, other = halves(value, place, 0)
    got = place.swap(other, "c", 1)
    pair = place.ordered("c", 1, mine, got)
    both = jnp.stack(pair, axis=1)
    return both.reshape(-1, both.shape[-1])


def own_devices(place, value, rows):
    shaped = value.reshape(place.chips // 2, 2, rows, value.shape[-1])
    mine = lax.dynamic_index_in_dim(shaped, place.at["c"], 1, keepdims=False)
    other = lax.dynamic_index_in_dim(shaped, 1 - place.at["c"], 1, keepdims=False)
    got = place.swap(other, "c", 1)
    return jnp.concatenate(place.ordered("c", 1, mine, got), axis=0)


def on_device(
    inputs,
    cotangent,
    segments,
    norm1_gain,
    input_proj,
    branch_proj,
    conv_weight,
    conv_bias,
    recur_gate,
    input_gate,
    recur_bias,
    input_bias,
    decay_param,
    output_proj,
    norm2_gain,
    mlp_gate,
    mlp_up,
    mlp_down,
):
    place = Place()
    core = place.at["c"]
    chips = place.chips
    rows_dev, group, model = inputs.shape
    n_rows = 2 * rows_dev
    tokens_dev = rows_dev * group
    tokens = 2 * tokens_dev
    d_rows, lru = input_proj.shape
    ffn = mlp_gate.shape[1]
    r_rows, block = recur_gate.shape
    f_rows = mlp_down.shape[0]
    lru_half, ffn_half = lru // 2, ffn // 2
    pair = lambda value: place.swap(value, "c", 1)

    vectors = jnp.concatenate(
        [
            norm1_gain,
            norm2_gain,
            conv_weight.reshape(-1),
            conv_bias,
            recur_bias,
            input_bias,
            decay_param,
        ]
    )
    small = vectors[None, None, None, None]
    for axis, dim in (("c", 3), ("x", 2), ("y", 1), ("z", 0)):
        small = place.gather(small, axis, dim)
    small = small.reshape(2 * chips, -1).astype(F32)
    gain_one = small[:, :d_rows].reshape(-1)
    gain_two = small[:, d_rows : 2 * d_rows].reshape(-1)
    vec = small[:, 2 * d_rows :].reshape(2 * chips, 8, r_rows)
    vec = jnp.transpose(vec, (1, 0, 2)).reshape(8, lru)
    vec = lax.dynamic_slice_in_dim(vec, core * lru_half, lru_half, 1)
    decay_raw = vec[7]
    vec = jnp.concatenate([vec[:7], 8.0 * jax.nn.softplus(decay_raw)[None]], axis=0)

    wide = [halves(w, place, 1) for w in (input_proj, branch_proj, mlp_gate, mlp_up)]
    mine = jnp.concatenate([w[0] for w in wide], axis=1)
    got = pair(jnp.concatenate([w[1] for w in wide], axis=1))
    chip_rows = jnp.concatenate(place.ordered("c", 1, mine, got), axis=0)
    gates = jnp.stack([recur_gate, input_gate]).reshape(-1, lru)
    gate_lines = gates.shape[0]
    group_a = jnp.concatenate([chip_rows[:, :lru], gates], axis=0)
    group_b = jnp.concatenate([output_proj, mlp_down], axis=0)
    group_c = chip_rows[:, lru:]

    a_left, a_right = gather_group(place, group_a, lru_half)
    chip_d = 2 * d_rows
    w_in = a_left[..., :chip_d, :].reshape(model, lru_half)
    w_branch = a_right[..., :chip_d, :].reshape(model, lru_half)
    packed = jnp.concatenate([a_left[..., chip_d:, :], a_right[..., chip_d:, :]], axis=-1)
    packed = packed.reshape(chips, 2, r_rows, block)
    packed = jnp.concatenate([packed[:, 0], packed[:, 1]], axis=-1)
    packed = own_channels(place, packed)
    gate_r, gate_i = packed[:, :block], packed[:, block:]

    b_left, b_right = gather_group(place, group_b, model // 2)
    outs = jnp.concatenate([b_left, b_right], axis=-1).reshape(chips, r_rows + f_rows, model)
    mine, other = halves(outs, place, 0)
    low_half, high_half = place.ordered("c", 1, mine, pair(other))
    w_out = jnp.stack([low_half[:, :r_rows], high_half[:, :r_rows]], axis=1).reshape(-1, model)
    w_down = jnp.stack([low_half[:, r_rows:], high_half[:, r_rows:]], axis=1).reshape(-1, model)

    c_left, c_right = gather_group(place, group_c, ffn_half)
    w_gate = c_left.reshape(model, ffn_half)
    w_up = c_right.reshape(model, ffn_half)

    flat = inputs.reshape(tokens_dev, model)
    first = normed(flat, gain_one).astype(BF)
    first = jnp.concatenate([first, pair(first)], axis=0)
    grad_out = cotangent.reshape(tokens_dev, model)
    grad_low = grad_out.astype(BF)
    grad_low = jnp.concatenate([grad_low, pair(grad_low)], axis=0)
    ids = jnp.concatenate([segments, pair(segments)], axis=0)
    prior_ids = place.along(ids[:, group - 3 :], 1)
    tail = first.reshape(n_rows, group, model)[:, group - 3 :]
    halo = place.along(tail, 1)
    halo = jnp.pad(halo, ((0, 0), (HALO - 3, 0), (0, 0))).reshape(n_rows * HALO, model)
    first_ext = jnp.concatenate([first, halo], axis=0)

    position = place.s * group + jnp.arange(group, dtype=jnp.int32)
    joined_ids = jnp.concatenate([prior_ids, ids], axis=1)
    marks = [(joined_ids[:, 2 : 2 + group] != ids) | (position == 0)[None, :]]
    for k in range(1, 4):
        marks.append(
            (joined_ids[:, 3 - k : 3 - k + group] == ids) & (position >= k)[None, :]
        )
    masks = jnp.stack(marks, axis=-1).astype(F32).reshape(tokens, 4)
    masks = jnp.pad(masks, ((0, 0), (0, 4)))

    mixer, conv, rpre, ipre, through, local, ends = forward_call(
        first_ext, w_in, vec, masks, gate_r, gate_i, n_rows, group
    )
    branch_pre = dot(first, w_branch)
    enter = carry_in(place, ends, 1)
    state, mixed, part = mix_call(local, through, enter, branch_pre, w_out, n_rows, group)
    middle = flat + (part[:tokens_dev] + pair(part[tokens_dev:]))
    second = normed(middle, gain_two).astype(BF)
    second = jnp.concatenate([second, pair(second)], axis=0)

    g_gate, g_up, g_down, part, back = ffn_call(second, grad_low, w_gate, w_up, w_down)
    result = middle + (part[:tokens_dev] + pair(part[tokens_dev:]))
    grad_second = back[:tokens_dev] + pair(back[tokens_dev:])
    grad_norm, grad_gain_two = jax.vjp(normed, middle, gain_two)[1](grad_second)
    grad_middle = grad_out + grad_norm
    mid_low = grad_middle.astype(BF)
    mid_low = jnp.concatenate([mid_low, pair(mid_low)], axis=0)

    g_out, g_branch, gbl, reach, local_back, ends_back = back_call(
        mid_low, w_out, branch_pre, state, rpre, mixed, vec, masks, first, n_rows, group
    )
    leave = carry_in(place, ends_back, -1)
    g_in, g_gate_r, g_gate_i, g_vec, grad_first = gates_call(
        reach, local_back, leave, state, enter, rpre, ipre, conv, mixer, vec, masks, gate_r, gate_i, first_ext, w_in, w_branch, gbl, n_rows, group
    )
    spill = grad_first[tokens:].reshape(n_rows, HALO, model)[:, HALO - 3 :]
    spill = place.along(spill, -1)
    spill = jnp.pad(spill, ((0, 0), (group - 3, 0), (0, 0))).reshape(tokens, model)
    grad_first = grad_first[:tokens] + spill
    grad_first = grad_first[:tokens_dev] + pair(grad_first[tokens_dev:])
    grad_norm, grad_gain_one = jax.vjp(normed, flat, gain_one)[1](grad_first)
    grad_inputs = grad_middle + grad_norm

    sum_c = scatter_group(
        place,
        g_gate.reshape(chips, chip_d, ffn_half),
        g_up.reshape(chips, chip_d, ffn_half),
    )
    outs = jnp.concatenate(
        [
            g_out.reshape(-1, r_rows, model),
            g_down.reshape(-1, f_rows, model),
        ],
        axis=1,
    )
    outs = own_devices(place, outs.reshape(-1, model), r_rows + f_rows)
    sum_b = scatter_group(place, outs[..., : model // 2], outs[..., model // 2 :])

    g_vec = g_vec * jnp.concatenate(
        [jnp.ones((7, lru_half), F32), -8.0 * jax.nn.sigmoid(decay_raw)[None]], axis=0
    )
    lines_r = jnp.concatenate([g_gate_r, g_gate_i], axis=1).astype(BF)
    lines_r = lines_r.reshape(chips, r_rows * 2 * block)
    lines_v = jnp.transpose(g_vec.reshape(8, chips, r_rows), (1, 0, 2)).astype(BF)
    lines_v = lines_v.reshape(chips, 8 * r_rows)
    packed = jnp.concatenate([lines_r, lines_v], axis=1)
    used = packed.shape[1]
    extra = -used % lru
    packed = jnp.pad(packed, ((0, 0), (0, extra)))
    packed = own_devices(place, packed, 1)
    packed = packed.reshape(chips, -1, lru)
    joined = jnp.concatenate(
        [
            jnp.concatenate([g_in, g_branch], axis=1).reshape(chips, chip_d, lru),
            packed,
        ],
        axis=1,
    )
    sum_a = scatter_group(place, joined[..., :lru_half], joined[..., lru_half:])

    gains = jnp.stack([grad_gain_one, grad_gain_two], axis=0)
    gains = jnp.transpose(gains.reshape(2, chips, 2, d_rows), (1, 2, 0, 3))
    gains = gains.reshape(
        place.size["z"], place.size["y"], place.size["x"], 2, 2 * d_rows
    )
    for axis, dim in (("c", 3), ("x", 2), ("y", 1), ("z", 0)):
        gains = place.scatter(gains, axis, dim, F32, F32)
    gains = gains.reshape(2, d_rows)

    summed = jnp.concatenate([sum_a[:chip_d], sum_c], axis=1)
    mine, other = halves(summed, place, 0)
    got = pair(other)
    low_half, high_half = place.ordered("c", 1, mine, got)

    def columns_of(start, width):
        span = slice(start, start + width)
        return jnp.concatenate([low_half[:, span], high_half[:, span]], axis=1)

    grad_input_proj = columns_of(0, lru_half)
    grad_branch_proj = columns_of(lru_half, lru_half)
    grad_gate = columns_of(lru, ffn_half)
    grad_up = columns_of(lru + ffn_half, ffn_half)
    own = sum_a[chip_d:].reshape(-1)[:used]
    own_gates = own[: r_rows * 2 * block].reshape(r_rows, 2 * block)
    own_vec = own[r_rows * 2 * block :].reshape(8, r_rows)
    return (
        result.reshape(inputs.shape),
        grad_inputs.reshape(inputs.shape),
        gains[0],
        grad_input_proj,
        grad_branch_proj,
        own_vec[:4],
        own_vec[4],
        own_gates[:, :block],
        own_gates[:, block:],
        own_vec[5],
        own_vec[6],
        own_vec[7],
        sum_b[:r_rows],
        gains[1],
        grad_gate,
        grad_up,
        sum_b[r_rows:],
    )


def solution(mesh):
    every = ("seq", "row")
    tokens, line, flat, taps = P("row", "seq", None), P(every, None), P(every), P(None, every)
    in_specs = (
        tokens,
        tokens,
        P("row", "seq"),
        flat,
        line,
        line,
        taps,
        flat,
        line,
        line,
        flat,
        flat,
        flat,
        line,
        flat,
        line,
        line,
        line,
    )
    out_specs = (
        tokens,
        tokens,
        flat,
        line,
        line,
        taps,
        flat,
        line,
        line,
        flat,
        flat,
        flat,
        line,
        flat,
        line,
        line,
        line,
    )
    return jax.shard_map(
        on_device, mesh=mesh, in_specs=in_specs, out_specs=out_specs, check_vma=False
    )
```

time: 1840 us -> 600 us (0.33)
  waiting for transfers between devices: 939 us -> 309 us
  local copies, waits for them, and re-layouts: 384 us -> 73.8 us
  blocking collectives: 205 us -> 0 us
  matrix products: 92.7 us -> 0.99 us
  other arithmetic: 142 us -> 60.6 us
  Pallas kernels: 0 us -> 60.7 us
  starting transfers between devices: 45.7 us -> 87.2 us
    reduce_scatter x6 -> x0, waiting for transfers between devices: 888 us -> none  [the longest x1 250 us: on_device(): lax.psum_scatter(row_term(second, paired), ('seq', 'row'), scatter_dimens...]
    ppermute x17 -> x74, waiting for transfers between devices: 47.7 us -> 309 us  [the longest x61 299 us: swap(): return lax.ppermute(value, AXES, pairs)]
    slice x102 -> x26, local copies, waits for them, and re-layouts: 206 us -> 12.6 us  [the longest x1 3.49 us: on_device(): sum_a = scatter_group(place, joined[..., :lru_half], joined[..., lru_half:])]
    all_gather x3 -> x0, blocking collectives: 121 us -> none  [the longest x1 42.7 us: on_device(): lax.all_gather(recur_gate, ('seq', 'row'), axis=0, tiled=True)]
    dot_general x22 -> x1, matrix products: 92.7 us -> 0.99 us  [dot(): return jnp.dot(a, b, preferred_element_type=F32)]
    pad x48 -> x1, local copies, waits for them, and re-layouts: 90.6 us -> 0.24 us  [on_device(): jnp.pad(spill, ((0, 0), (group - 3, 0), (0, 0))).reshape(tokens, model)]
    unnamed x2 -> x0, blocking collectives: 83.9 us -> none
    pallas_call x0 -> x5, Pallas kernels: none -> 60.7 us  [the longest x1 25.5 us: ffn_call(): pl.pallas_call(ffn_kernel, grid=(width // TILE,), in_specs=[full((tokens,...]
  transfers between devices with their start and end apart: 30 -> 74, of which waited for: 21 -> 32; matrix products, arithmetic and copies ran while one was open for 18% -> 19% of each run, Pallas kernels for 0% -> 6%
where the time goes in v1:
time: 600 us; the launch traced here: 596 us
  waiting for transfers between devices  309 us (52%)
  starting transfers between devices  87.2 us (15%)
  local copies, waits for them, and re-layouts  73.8 us (12%)
  Pallas kernels  60.7 us (10%)
  other arithmetic  60.6 us (10%)
    ppermute x61, waiting for transfers between devices, swap(): return lax.ppermute(value, AXES, pairs)  299 us
    ppermute x61, starting transfers between devices, swap(): return lax.ppermute(value, AXES, pairs)  58.9 us
    ppermute x13, starting transfers between devices, along(): return lax.ppermute(value, AXES, pairs)  28.3 us
    pallas_call x1, Pallas kernels, ffn_call(): pl.pallas_call(ffn_kernel, grid=(width // TILE,), in_specs=[full((tokens,...  25.5 us
    unnamed x197, local copies, waits for them, and re-layouts  23.5 us
    pallas_call x1, Pallas kernels, gates_call(): pl.pallas_call(functools.partial(gates_kernel, n_rows, group, block), gri...  16.1 us
    select_n x28, other arithmetic, ordered(): return (jnp.where(high, other, mine), jnp.where(high, mine, other))  13.9 us
    convert_element_type x15, other arithmetic, scatter(): (keep.astype(F32) + other.astype(F32)).astype(between if distance else dt...  13.5 us
  transfers between devices with their start and end apart: 74, of which 32 were waited for; matrix products, arithmetic and copies ran while one was open for 19% of the time, Pallas kernels for 6%

profile of v1, /device:TPU:0, one launch (start us, length us, event | category | flops | bytes accessed | tf_op | source)
XLA Modules:
  0.0 595.5 jit_solution(6663798867662028829)
XLA Ops:
  2.6 3.0 collective-permute-start.22
  12.5 3.4 collective-permute-start.13
  17.4 2.3 collective-permute-start.2
  25.2 4.1 collective-permute-start.4
  34.3 3.0 collective-permute-start.23
  40.6 15.2 %collective-permute-done.8 = bf16[1,1,1,72,1536]{4,3,2,1,0:T(8,128)(2,1)S(1)} collective-permute-done((bf16[1,1,1,72,1536]{4,3,2,1,0:T(8,128)(2,1)S(1)}, bf16[1,1,1,72,1536]{4,3,2,1,0:T(8,128)(2,1)S(1)}, u32[]{:S(2)}, u32[]{:S(2)}) %collective-permute-start.8) | collective-permute-done | bytes 221216 | tf_op jit(solution)/shard_map/ppermute | solution.py:38
  57.3 3.1 collective-permute-start.6
  62.6 4.5 collective-permute-done.32
  67.2 15.2 %collective-permute-done.9 = bf16[2,1,1,72,1536]{4,3,2,1,0:T(8,128)(2,1)S(1)} collective-permute-done((bf16[2,1,1,72,1536]{4,3,2,1,0:T(8,128)(2,1)S(1)}, bf16[2,1,1,72,1536]{4,3,2,1,0:T(8,128)(2,1)S(1)}, u32[]{:S(2)}, u32[]{:S(2)}) %collective-permute-start.9) | collective-permute-done | bytes 442400 | tf_op jit(solution)/shard_map/ppermute | solution.py:38
  83.2 2.8 collective-permute-start.33
  89.8 5.8 collective-permute-done.14
  96.7 2.6 collective-permute-done.10
  101.0 18.4 %collective-permute-done.33 = bf16[2,1,1,64,3072]{4,3,2,1,0:T(8,128)(2,1)S(1)} collective-permute-done((bf16[2,1,1,64,3072]{4,3,2,1,0:T(8,128)(2,1)S(1)}, bf16[2,1,1,64,3072]{4,3,2,1,0:T(8,128)(2,1)S(1)}, u32[]{:S(2)}, u32[]{:S(2)}) %collective-permute-start.33) | collective-permute-done | bytes 786464 | tf_op jit(solution)/shard_map/ppermute | solution.py:38
  125.3 18.8 %collective-permute-done.36 = bf16[4,1,1,64,1536]{4,3,2,1,0:T(8,128)(2,1)S(1)} collective-permute-done((bf16[4,1,1,64,1536]{4,3,2,1,0:T(8,128)(2,1)S(1)}, bf16[4,1,1,64,1536]{4,3,2,1,0:T(8,128)(2,1)S(1)}, u32[]{:S(2)}, u32[]{:S(2)}) %collective-permute-start.36) | collective-permute-done | bytes 786464 | tf_op jit(solution)/shard_map/ppermute | solution.py:38
  146.8 23.5 %collective-permute-done.34 = bf16[4,1,1,64,1536]{4,3,2,1,0:T(8,128)(2,1)S(1)} collective-permute-done((bf16[4,1,1,64,1536]{4,3,2,1,0:T(8,128)(2,1)S(1)}, bf16[4,1,1,64,1536]{4,3,2,1,0:T(8,128)(2,1)S(1)}, u32[]{:S(2)}, u32[]{:S(2)}) %collective-permute-start.34) | collective-permute-done | bytes 786464 | tf_op jit(solution)/shard_map/ppermute | solution.py:38
  183.5 8.7 %recurrence_forward.1 = (bf16[544,768]{1,0:T(8,128)(2,1)S(1)}, bf16[512,768]{1,0:T(8,128)(2,1)S(1)}, f32[512,768]{1,0:T(8,128)S(1)}, f32[512,768]{1,0:T(8,128)S(...) custom-call(bf16[544,1024]{1,0:T(8,128)(2,1)S(1)} %pad_maximum_fusion.11.first_ref, ...), custom_call_target="tpu_custom_call" | custom-call | tf_op jit(solution)/shard_map/recurrence_forward/pallas_call | solution.py:268
  194.1 4.1 collective-permute-start.17
  198.2 3.0 collective-permute-start.18
  205.0 3.4 collective-permute-start.20
  214.6 3.1 mix.1
  220.2 18.8 %collective-permute-done.35 = bf16[4,2,1,64,1536]{4,3,2,1,0:T(8,128)(2,1)S(1)} collective-permute-done((bf16[4,2,1,64,1536]{4,3,2,1,0:T(8,128)(2,1)S(1)}, bf16[4,2,1,64,1536]{4,3,2,1,0:T(8,128)(2,1)S(1)}, u32[]{:S(2)}, u32[]{:S(2)}) %collective-permute-start.35) | collective-permute-done | bytes 1572896 | tf_op jit(solution)/shard_map/ppermute | solution.py:38
  246.6 25.5 %feed_forward.1 = (bf16[1024,1536]{1,0:T(8,128)(2,1)S(1)}, bf16[1024,1536]{1,0:T(8,128)(2,1)S(1)}, bf16[1536,1024]{1,0:T(8,128)(2,1)}, f32[512,1024]{1,0:T(8,128)S(1)}, f32[512,1024]{1,0:T(8,128)S(1)}) custom-call(bf16[512,1024]{1,0:T(8,128)(2,1)S(1)} %pad_maximum_fusion.13.second_ref, bf16[512,1024]{1,0:T(8,128)(2,1)S(1)} %copy-done.14, ...), custom_call_target="tpu_custom_call" | custom-call | tf_op jit(solution)/shard_map/feed_forward/pallas_call | solution.py:376
  278.5 2.8 constant_dynamic-slice_fusion.8
  287.5 3.4 fusion.53
  291.0 2.2 collective-permute-done.40
  299.7 7.3 %recurrence_back.1 = (bf16[768,1024]{1,0:T(8,128)(2,1)S(1)}, bf16[1024,768]{1,0:T(8,128)(2,1)S(1)}, bf16[512,768]{1,0:T(8,128)(2,1)S(1)}, f32[512,768]{1,0:T(8,1...) custom-call(bf16[512,1024]{1,0:T(8,128)(2,1)S(1)} %pad_maximum_fusion.15.low_ref, bf16[768,1024]{1,0:T(8,128)(2,1)S(1)} %bitcast.158, ...), custom_call_target="tpu_custom_call" | custom-call | tf_op jit(solution)/shard_map/recurrence_back/pallas_call | solution.py:461
  311.0 7.9 %collective-permute-done.62 = bf16[4,1,2,64,1536]{4,3,2,1,0:T(8,128)(2,1)} collective-permute-done((bf16[4,1,2,64,1536]{4,3,2,1,0:T(8,128)(2,1)}, bf16[4,1,2,64,1536]{4,3,2,1,0:T(8,128)(2,1)}, u32[]{:S(2)}, u32[]{:S(2)}) %collective-permute-start.62) | collective-permute-done | bytes 1572896 | tf_op jit(solution)/shard_map/ppermute | solution.py:38
  333.1 2.3 collective-permute-done.44
  335.4 4.0 collective-permute-done.45
  339.4 16.1 %recurrence_gates.1 = (bf16[1024,768]{1,0:T(8,128)(2,1)S(1)}, f32[768,128]{1,0:T(8,128)S(1)}, f32[768,128]{1,0:T(8,128)S(1)}, f32[8,768]{1,0:T(8,128)S(1)}, f32[544,1024]{1,0:T(8,128)}) custom-call(f32[512,768]{1,0:T(8,128)S(1)} %get-tuple-element.52.reach_ref, f32[512,768]{1,0:T(8,128)S(1)} %get-tuple-element.53.local_ref, f32[4,768]{1,0:T(4,128)S(1)} %fusion.32.leave_ref, ...), custom_call_target="tpu_custom_call" | custom-call | tf_op jit(solution)/shard_map/recurrence_gates/pallas_call | solution.py:617
  359.8 3.4 copy_dynamic-update-slice_fusion
  368.3 3.5 fusion.55
  373.4 3.6 constant_dynamic-slice_fusion.14
  379.5 4.1 reshape.272
  383.6 4.9 constant_dynamic-slice_fusion.17
  396.0 16.0 %collective-permute-done.49 = f32[4,2,1,1,64]{4,3,2,1,0:T(1,128)S(1)} collective-permute-done((f32[4,2,1,1,64]{4,3,2,1,0:T(1,128)S(1)}, f32[4,2,1,1,64]{4,3,2,1,0:T(1,128)S(1)}, u32[]{:S(2)}, u32[]{:S(2)}) %collective-permute-start.49) | collective-permute-done | bytes 2080 | tf_op jit(solution)/shard_map/ppermute | solution.py:38
  412.9 2.8 collective-permute-done.50
  415.9 32.9 %collective-permute-done.51 = f32[2,1,1,1,64]{4,3,2,1,0:T(1,128)S(1)} collective-permute-done((f32[2,1,1,1,64]{4,3,2,1,0:T(1,128)S(1)}, f32[2,1,1,1,64]{4,3,2,1,0:T(1,128)S(1)}, u32[]{:S(2)}, u32[]{:S(2)}) %collective-permute-start.51) | collective-permute-done | bytes 544 | tf_op jit(solution)/shard_map/ppermute | solution.py:38
  450.2 2.2 collective-permute-done.52
  458.6 6.3 %collective-permute-done.57 = bf16[4,1,1,73,768]{4,0,3,2,1:T(4,128)(2,1)S(1)} collective-permute-done((bf16[4,1,1,73,768]{4,0,3,2,1:T(4,128)(2,1)S(1)}, bf16[4,1,1,73,768]{4,0,3,2,1:T(4,128)(2,1)S(1)}, u32[]{:S(2)}, u32[]{:S(2)}) %collective-permute-start.57) | collective-permute-done | bytes 448544 | tf_op jit(solution)/shard_map/ppermute | solution.py:38
  469.8 18.2 %collective-permute-done.58 = bf16[2,1,1,73,1536]{4,0,3,2,1:T(2,128)(2,1)S(1)} collective-permute-done((bf16[2,1,1,73,1536]{4,0,3,2,1:T(2,128)(2,1)S(1)}, bf16[2,1,1,73,1536]{4,0,3,2,1:T(2,128)(2,1)S(1)}, u32[]{:S(2)}, u32[]{:S(2)}) %collective-permute-start.58) | collective-permute-done | bytes 448544 | tf_op jit(solution)/shard_map/ppermute | solution.py:38
  489.4 11.3 %collective-permute-done.59 = bf16[1,1,1,73,1536]{4,0,3,2,1:T(2,128)(2,1)S(1)} collective-permute-done((bf16[1,1,1,73,1536]{4,0,3,2,1:T(2,128)(2,1)S(1)}, bf16[1,1,1,73,1536]{4,0,3,2,1:T(2,128)(2,1)S(1)}, u32[]{:S(2)}, u32[]{:S(2)}) %collective-permute-start.59) | collective-permute-done | bytes 224288 | tf_op jit(solution)/shard_map/ppermute | solution.py:38
  506.6 3.4 broadcast_select_fusion
  510.8 2.2 collective-permute-start.70
  515.9 23.6 %collective-permute-done.70 = bf16[4,1,2,144,512]{4,3,2,1,0:T(8,128)(2,1)S(1)} collective-permute-done((bf16[4,1,2,144,512]{4,3,2,1,0:T(8,128)(2,1)S(1)}, bf16[4,1,2,144,512]{4,3,2,1,0:T(8,128)(2,1)S(1)}, u32[]{:S(2)}, u32[]{:S(2)}) %collective-permute-start.70) | collective-permute-done | bytes 1179680 | tf_op jit(solution)/shard_map/ppermute | solution.py:38
  543.9 11.3 %collective-permute-done.71 = bf16[4,1,1,144,512]{4,3,2,1,0:T(8,128)(2,1)S(1)} collective-permute-done((bf16[4,1,1,144,512]{4,3,2,1,0:T(8,128)(2,1)S(1)}, bf16[4,1,1,144,512]{4,3,2,1,0:T(8,128)(2,1)S(1)}, u32[]{:S(2)}, u32[]{:S(2)}) %collective-permute-start.71) | collective-permute-done | bytes 589856 | tf_op jit(solution)/shard_map/ppermute | solution.py:38
  560.1 24.4 %collective-permute-done.72 = bf16[2,1,1,144,1024]{4,3,2,1,0:T(8,128)(2,1)S(1)} collective-permute-done((bf16[2,1,1,144,1024]{4,3,2,1,0:T(8,128)(2,1)S(1)}, bf16[2,1,1,144,1024]{4,3,2,1,0:T(8,128)(2,1)S(1)}, u32[]{:S(2)}, u32[]{:S(2)}) %collective-permute-start.72) | collective-permute-done | bytes 589856 | tf_op jit(solution)/shard_map/ppermute | solution.py:38
  585.6 8.1 %collective-permute-done.73 = bf16[1,1,1,144,1024]{4,3,2,1,0:T(8,128)(2,1)S(1)} collective-permute-done((bf16[1,1,1,144,1024]{4,3,2,1,0:T(8,128)(2,1)S(1)}, bf16[1,1,1,144,1024]{4,3,2,1,0:T(8,128)(2,1)S(1)}, u32[]{:S(2)}, u32[]{:S(2)}) %collective-permute-start.73) | collective-permute-done | bytes 294944 | tf_op jit(solution)/shard_map/ppermute | solution.py:38
  (529 shorter events, 171.7 us)
Async XLA Ops:
  2.6 30.6 %collective-permute-start.22 = (bf16[1,1,1,144,1024]{4,3,2,1,0:T(8,128)(2,1)}, bf16[1,1,1,144,1024]{4,3,2,1,0:T(8,128)(2,1)}, u32[]{:S(2)}, u32[]{:S(2)}) collective-permute-start(bf16[1,1,1,144,1024]{4,3,2,1,0:T(8,128)(2,1)} %maximum_bitcast_fusion), channel_id=1, source_target_pairs={{0,8},{1,9},{2,10},{3,11},{4,12},{5,13},{6,14},{7,15},{8,0},{9,1},... | collective-permute-start | bytes 884744 | tf_op jit(solution)/shard_map/ppermute | solution.py:38
  9.0 28.3 %collective-permute-start.7 = (bf16[32,4608]{1,0:T(8,128)(2,1)}, bf16[32,4608]{1,0:T(8,128)(2,1)}, u32[]{:S(2)}, u32[]{:S(2)}) collective-permute-start(bf16[32,4608]{1,0:T(8,128)(2,1)} %pad_maximum_fusion.32), channel_id=1, source_target_pairs={{0,1},{1,0},{2,3},{3,2},{4,5},{5,4},{6,7},{7,6},{8,9},{9,8},{10,11... | collective-permute-start | bytes 884744 | tf_op jit(solution)/shard_map/ppermute | solution.py:38
  9.9 50.5 %collective-permute-start.31 = (bf16[256,1024]{1,0:T(8,128)(2,1)S(1)}, bf16[256,1024]{1,0:T(8,128)(2,1)}, u32[]{:S(2)}, u32[]{:S(2)}) collective-permute-start(bf16[256,1024]{1,0:T(8,128)(2,1)S(1)} %bitcast_convert_fusion), channel_id=1, source_target_pairs={{0,1},{1,0},{2,3},{3,2},{4,5},{5,4},{6,7},{7,6},{8,9},{9,8},{10,11... | collective-permute-start | bytes 1572872 | tf_op jit(solution)/shard_map/ppermute | solution.py:38
  32.1 25.1 %collective-permute-start.5 = (bf16[256,1024]{1,0:T(8,128)(2,1)S(1)}, bf16[256,1024]{1,0:T(8,128)(2,1)S(1)}, u32[]{:S(2)}, u32[]{:S(2)}) collective-permute-start(bf16[256,1024]{1,0:T(8,128)(2,1)S(1)} %multiply_convert_fusion.1), channel_id=1, source_target_pairs={{0,1},{1,0},{2,3},{3,2},{4,5},{5,4},{6,7},{7,6},{8,9},{9,8},{10,11... | collective-permute-start | bytes 1572872 | tf_op jit(solution)/shard_map/ppermute | solution.py:38
  34.3 51.7 %collective-permute-start.23 = (bf16[2,1,1,144,1024]{4,3,2,1,0:T(8,128)(2,1)S(1)}, bf16[2,1,1,144,1024]{4,3,2,1,0:T(8,128)(2,1)S(1)}, u32[]{:S(2)}, u32[]{:S(2)}) collective-permute-start(bf16[2,1,1,144,1024]{4,3,2,1,0:T(8,128)(2,1)S(1)} %pad_maximum_fusion.21), channel_id=1, source_target_pairs={{0,16},{1,17},{2,18},{3,19},{4,20},{5,21},{6,22},{7,23},{8,24},{9,... | collective-permute-start | bytes 1769480 | tf_op jit(solution)/shard_map/ppermute | solution.py:38
  38.4 17.4 %collective-permute-start.8 = (bf16[1,1,1,72,1536]{4,3,2,1,0:T(8,128)(2,1)S(1)}, bf16[1,1,1,72,1536]{4,3,2,1,0:T(8,128)(2,1)S(1)}, u32[]{:S(2)}, u32[]{:S(2)}) collective-permute-start(bf16[1,1,1,72,1536]{4,3,2,1,0:T(8,128)(2,1)S(1)} %fusion.26), channel_id=1, source_target_pairs={{0,8},{1,9},{2,10},{3,11},{4,12},{5,13},{6,14},{7,15},{8,0},{9,1},... | collective-permute-start | bytes 663560 | tf_op jit(solution)/shard_map/ppermute | solution.py:38
  39.0 28.2 %collective-permute-start.32 = (bf16[1,1,1,64,3072]{4,3,2,1,0:T(8,128)(2,1)S(1)}, bf16[1,1,1,64,3072]{4,3,2,1,0:T(8,128)(2,1)S(1)}, u32[]{:S(2)}, u32[]{:S(2)}) collective-permute-start(bf16[1,1,1,64,3072]{4,3,2,1,0:T(8,128)(2,1)S(1)} %fusion.23), channel_id=1, source_target_pairs={{0,8},{1,9},{2,10},{3,11},{4,12},{5,13},{6,14},{7,15},{8,0},{9,1},... | collective-permute-start | bytes 1179656 | tf_op jit(solution)/shard_map/ppermute | solution.py:38
  55.9 26.5 %collective-permute-start.9 = (bf16[2,1,1,72,1536]{4,3,2,1,0:T(8,128)(2,1)S(1)}, bf16[2,1,1,72,1536]{4,3,2,1,0:T(8,128)(2,1)S(1)}, u32[]{:S(2)}, u32[]{:S(2)}) collective-permute-start(bf16[2,1,1,72,1536]{4,3,2,1,0:T(8,128)(2,1)S(1)} %pad_maximum_fusion.23), channel_id=1, source_target_pairs={{0,16},{1,17},{2,18},{3,19},{4,20},{5,21},{6,22},{7,23},{8,24},{9,... | collective-permute-start | bytes 1327112 | tf_op jit(solution)/shard_map/ppermute | solution.py:38
  82.6 13.1 %collective-permute-start.14 = (bf16[4,1,1,72,768]{4,3,2,1,0:T(8,128)(2,1)S(1)}, bf16[4,1,1,72,768]{4,3,2,1,0:T(8,128)(2,1)S(1)}, u32[]{:S(2)}, u32[]{:S(2)}) collective-permute-start(bf16[4,1,1,72,768]{4,3,2,1,0:T(8,128)(2,1)S(1)} %get-tuple-element.122), channel_id=1, source_target_pairs={{0,2},{1,3},{2,0},{3,1},{4,6},{5,7},{6,4},{7,5},{8,10},{9,11},{10,... | collective-permute-start | bytes 1327112 | tf_op jit(solution)/shard_map/ppermute | solution.py:38
  83.2 36.2 %collective-permute-start.33 = (bf16[2,1,1,64,3072]{4,3,2,1,0:T(8,128)(2,1)S(1)}, bf16[2,1,1,64,3072]{4,3,2,1,0:T(8,128)(2,1)S(1)}, u32[]{:S(2)}, u32[]{:S(2)}) collective-permute-start(bf16[2,1,1,64,3072]{4,3,2,1,0:T(8,128)(2,1)S(1)} %pad_maximum_fusion.19), channel_id=1, source_target_pairs={{0,16},{1,17},{2,18},{3,19},{4,20},{5,21},{6,22},{7,23},{8,24},{9,... | collective-permute-start | bytes 2359304 | tf_op jit(solution)/shard_map/ppermute | solution.py:38
  86.1 13.2 %collective-permute-start.10 = (bf16[4,1,1,72,768]{4,3,2,1,0:T(8,128)(2,1)S(1)}, bf16[4,1,1,72,768]{4,3,2,1,0:T(8,128)(2,1)S(1)}, u32[]{:S(2)}, u32[]{:S(2)}) collective-permute-start(bf16[4,1,1,72,768]{4,3,2,1,0:T(8,128)(2,1)S(1)} %get-tuple-element.123), channel_id=1, source_target_pairs={{0,4},{1,5},{2,6},{3,7},{4,0},{5,1},{6,2},{7,3},{8,12},{9,13},{10,... | collective-permute-start | bytes 1327112 | tf_op jit(solution)/shard_map/ppermute | solution.py:38
  86.3 34.9 %collective-permute-start.24 = (bf16[4,1,1,144,512]{4,3,2,1,0:T(8,128)(2,1)S(1)}, bf16[4,1,1,144,512]{4,3,2,1,0:T(8,128)(2,1)S(1)}, u32[]{:S(2)}, u32[]{:S(2)}) collective-permute-start(bf16[4,1,1,144,512]{4,3,2,1,0:T(8,128)(2,1)S(1)} %get-tuple-element.113), channel_id=1, source_target_pairs={{0,4},{1,5},{2,6},{3,7},{4,0},{5,1},{6,2},{7,3},{8,12},{9,13},{10,... | collective-permute-start | bytes 1769480 | tf_op jit(solution)/shard_map/ppermute | solution.py:38
  88.4 34.8 %collective-permute-start.26 = (bf16[4,1,1,144,512]{4,3,2,1,0:T(8,128)(2,1)S(1)}, bf16[4,1,1,144,512]{4,3,2,1,0:T(8,128)(2,1)S(1)}, u32[]{:S(2)}, u32[]{:S(2)}) collective-permute-start(bf16[4,1,1,144,512]{4,3,2,1,0:T(8,128)(2,1)S(1)} %get-tuple-element.114), channel_id=1, source_target_pairs={{0,2},{1,3},{2,0},{3,1},{4,6},{5,7},{6,4},{7,5},{8,10},{9,11},{10,... | collective-permute-start | bytes 1769480 | tf_op jit(solution)/shard_map/ppermute | solution.py:38
  95.8 75.8 %collective-permute-start.15 = (bf16[4,1,2,72,768]{4,3,2,1,0:T(8,128)(2,1)S(1)}, bf16[4,1,2,72,768]{4,3,2,1,0:T(8,128)(2,1)S(1)}, u32[]{:S(2)}, u32[]{:S(2)}) collective-permute-start(bf16[4,1,2,72,768]{4,3,2,1,0:T(8,128)(2,1)S(1)} %pad_maximum_fusion.17), channel_id=1, source_target_pairs={{0,4},{1,5},{2,6},{3,7},{4,0},{5,1},{6,2},{7,3},{8,12},{9,13},{10,... | collective-permute-start | bytes 2654216 | tf_op jit(solution)/shard_map/ppermute | solution.py:38
  99.4 72.3 %collective-permute-start.11 = (bf16[4,2,1,72,768]{4,3,2,1,0:T(8,128)(2,1)S(1)}, bf16[4,2,1,72,768]{4,3,2,1,0:T(8,128)(2,1)S(1)}, u32[]{:S(2)}, u32[]{:S(2)}) collective-permute-start(bf16[4,2,1,72,768]{4,3,2,1,0:T(8,128)(2,1)S(1)} %pad_maximum_fusion.16), channel_id=1, source_target_pairs={{0,2},{1,3},{2,0},{3,1},{4,6},{5,7},{6,4},{7,5},{8,10},{9,11},{10,... | collective-permute-start | bytes 2654216 | tf_op jit(solution)/shard_map/ppermute | solution.py:38
  119.6 24.5 %collective-permute-start.36 = (bf16[4,1,1,64,1536]{4,3,2,1,0:T(8,128)(2,1)S(1)}, bf16[4,1,1,64,1536]{4,3,2,1,0:T(8,128)(2,1)S(1)}, u32[]{:S(2)}, u32[]{:S(2)}) collective-permute-start(bf16[4,1,1,64,1536]{4,3,2,1,0:T(8,128)(2,1)S(1)} %get-tuple-element.105), channel_id=1, source_target_pairs={{0,2},{1,3},{2,0},{3,1},{4,6},{5,7},{6,4},{7,5},{8,10},{9,11},{10,... | collective-permute-start | bytes 2359304 | tf_op jit(solution)/shard_map/ppermute | solution.py:38
  122.6 55.1 %collective-permute-start.25 = (bf16[4,2,1,144,512]{4,3,2,1,0:T(8,128)(2,1)}, bf16[4,2,1,144,512]{4,3,2,1,0:T(8,128)(2,1)}, u32[]{:S(2)}, u32[]{:S(2)}) collective-permute-start(bf16[4,2,1,144,512]{4,3,2,1,0:T(8,128)(2,1)} %pad_maximum_fusion.9), channel_id=1, source_target_pairs={{0,2},{1,3},{2,0},{3,1},{4,6},{5,7},{6,4},{7,5},{8,10},{9,11},{10,... | collective-permute-start | bytes 3538952 | tf_op jit(solution)/shard_map/ppermute | solution.py:38
  124.5 56.0 %collective-permute-start.27 = (bf16[4,1,2,144,512]{4,3,2,1,0:T(8,128)(2,1)}, bf16[4,1,2,144,512]{4,3,2,1,0:T(8,128)(2,1)}, u32[]{:S(2)}, u32[]{:S(2)}) collective-permute-start(bf16[4,1,2,144,512]{4,3,2,1,0:T(8,128)(2,1)} %pad_maximum_fusion.10), channel_id=1, source_target_pairs={{0,4},{1,5},{2,6},{3,7},{4,0},{5,1},{6,2},{7,3},{8,12},{9,13},{10,... | collective-permute-start | bytes 3538952 | tf_op jit(solution)/shard_map/ppermute | solution.py:38
  144.1 26.2 %collective-permute-start.34 = (bf16[4,1,1,64,1536]{4,3,2,1,0:T(8,128)(2,1)S(1)}, bf16[4,1,1,64,1536]{4,3,2,1,0:T(8,128)(2,1)S(1)}, u32[]{:S(2)}, u32[]{:S(2)}) collective-permute-start(bf16[4,1,1,64,1536]{4,3,2,1,0:T(8,128)(2,1)S(1)} %get-tuple-element.106), channel_id=1, source_target_pairs={{0,4},{1,5},{2,6},{3,7},{4,0},{5,1},{6,2},{7,3},{8,12},{9,13},{10,... | collective-permute-start | bytes 2359304 | tf_op jit(solution)/shard_map/ppermute | solution.py:38
  170.3 42.0 %collective-permute-start.37 = (bf16[4,1,2,64,1536]{4,3,2,1,0:T(8,128)(2,1)}, bf16[4,1,2,64,1536]{4,3,2,1,0:T(8,128)(2,1)}, u32[]{:S(2)}, u32[]{:S(2)}) collective-permute-start(bf16[4,1,2,64,1536]{4,3,2,1,0:T(8,128)(2,1)} %pad_maximum_fusion.8), channel_id=1, source_target_pairs={{0,4},{1,5},{2,6},{3,7},{4,0},{5,1},{6,2},{7,3},{8,12},{9,13},{10,... | collective-permute-start | bytes 4718600 | tf_op jit(solution)/shard_map/ppermute | solution.py:38
  182.9 31.0 %collective-permute-start.28 = (bf16[8,144,1024]{2,1,0:T(8,128)(2,1)S(1)}, bf16[8,144,1024]{2,1,0:T(8,128)(2,1)S(1)}, u32[]{:S(2)}, u32[]{:S(2)}) collective-permute-start(bf16[8,144,1024]{2,1,0:T(8,128)(2,1)S(1)} %constant_dynamic-slice_fusion.30), channel_id=1, source_target_pairs={{0,1},{1,0},{2,3},{3,2},{4,5},{5,4},{6,7},{7,6},{8,9},{9,8},{10,11... | collective-permute-start | bytes 7077896 | tf_op jit(solution)/shard_map/ppermute | solution.py:38
  203.3 35.6 %collective-permute-start.35 = (bf16[4,2,1,64,1536]{4,3,2,1,0:T(8,128)(2,1)S(1)}, bf16[4,2,1,64,1536]{4,3,2,1,0:T(8,128)(2,1)S(1)}, u32[]{:S(2)}, u32[]{:S(2)}) collective-permute-start(bf16[4,2,1,64,1536]{4,3,2,1,0:T(8,128)(2,1)S(1)} %pad_maximum_fusion.7), channel_id=1, source_target_pairs={{0,2},{1,3},{2,0},{3,1},{4,6},{5,7},{6,4},{7,5},{8,10},{9,11},{10,... | collective-permute-start | bytes 4718600 | tf_op jit(solution)/shard_map/ppermute | solution.py:38
  217.8 23.4 %collective-permute-start.29 = (f32[256,1024]{1,0:T(8,128)S(1)}, f32[256,1024]{1,0:T(8,128)S(1)}, u32[]{:S(2)}, u32[]{:S(2)}) collective-permute-start(f32[256,1024]{1,0:T(8,128)S(1)} %slice.327), channel_id=1, source_target_pairs={{0,1},{1,0},{2,3},{3,2},{4,5},{5,4},{6,7},{7,6},{8,9},{9,8},{10,11... | collective-permute-start | bytes 3145736 | tf_op jit(solution)/shard_map/ppermute | solution.py:38
  281.3 37.7 %collective-permute-start.62 = (bf16[4,1,2,64,1536]{4,3,2,1,0:T(8,128)(2,1)}, bf16[4,1,2,64,1536]{4,3,2,1,0:T(8,128)(2,1)}, u32[]{:S(2)}, u32[]{:S(2)}) collective-permute-start(bf16[4,1,2,64,1536]{4,3,2,1,0:T(8,128)(2,1)} %constant_dynamic-slice_fusion.8), channel_id=1, source_target_pairs={{0,4},{1,5},{2,6},{3,7},{4,0},{5,1},{6,2},{7,3},{8,12},{9,13},{10,... | collective-permute-start | bytes 4718600 | tf_op jit(solution)/shard_map/ppermute | solution.py:38
  284.4 39.2 %collective-permute-start.60 = (bf16[4,2,1,64,1536]{4,3,2,1,0:T(8,128)(2,1)}, bf16[4,2,1,64,1536]{4,3,2,1,0:T(8,128)(2,1)}, u32[]{:S(2)}, u32[]{:S(2)}) collective-permute-start(bf16[4,2,1,64,1536]{4,3,2,1,0:T(8,128)(2,1)} %constant_dynamic-slice_fusion.10), channel_id=1, source_target_pairs={{0,2},{1,3},{2,0},{3,1},{4,6},{5,7},{6,4},{7,5},{8,10},{9,11},{10,... | collective-permute-start | bytes 4718600 | tf_op jit(solution)/shard_map/ppermute | solution.py:38
  307.0 21.7 %collective-permute-start.41 = (f32[8,768]{1,0:T(8,128)S(1)}, f32[8,768]{1,0:T(8,128)S(1)}, u32[]{:S(2)}, u32[]{:S(2)}) collective-permute-start(f32[8,768]{1,0:T(8,128)S(1)} %get-tuple-element.54), channel_id=1, source_target_pairs={{12,0},{13,1},{14,2},{15,3},{16,4},{17,5},{18,6},{19,7},{20,8},{21... | collective-permute-start | bytes 73736 | tf_op jit(solution)/shard_map/ppermute | solution.py:46
  308.3 20.4 %collective-permute-start.42 = (f32[8,768]{1,0:T(8,128)S(1)}, f32[8,768]{1,0:T(8,128)S(1)}, u32[]{:S(2)}, u32[]{:S(2)}) collective-permute-start(f32[8,768]{1,0:T(8,128)S(1)} %get-tuple-element.54), channel_id=1, source_target_pairs={{8,0},{9,1},{10,2},{11,3},{12,4},{13,5},{14,6},{15,7},{16,8},{17,9... | collective-permute-start | bytes 73736 | tf_op jit(solution)/shard_map/ppermute | solution.py:46
  309.6 19.1 %collective-permute-start.43 = (f32[8,768]{1,0:T(8,128)S(1)}, f32[8,768]{1,0:T(8,128)S(1)}, u32[]{:S(2)}, u32[]{:S(2)}) collective-permute-start(f32[8,768]{1,0:T(8,128)S(1)} %get-tuple-element.54), channel_id=1, source_target_pairs={{4,0},{5,1},{6,2},{7,3},{8,4},{9,5},{10,6},{11,7},{12,8},{13,9},{1... | collective-permute-start | bytes 73736 | tf_op jit(solution)/shard_map/ppermute | solution.py:46
  322.0 69.6 %collective-permute-start.63 = (bf16[4,1,1,64,1536]{4,3,2,1,0:T(8,128)(2,1)}, bf16[4,1,1,64,1536]{4,3,2,1,0:T(8,128)(2,1)}, u32[]{:S(2)}, u32[]{:S(2)}) collective-permute-start(bf16[4,1,1,64,1536]{4,3,2,1,0:T(8,128)(2,1)} %constant_dynamic-slice_fusion.7), channel_id=1, source_target_pairs={{0,2},{1,3},{2,0},{3,1},{4,6},{5,7},{6,4},{7,5},{8,10},{9,11},{10,... | collective-permute-start | bytes 2359304 | tf_op jit(solution)/shard_map/ppermute | solution.py:38
  326.6 67.9 %collective-permute-start.61 = (bf16[4,1,1,64,1536]{4,3,2,1,0:T(8,128)(2,1)}, bf16[4,1,1,64,1536]{4,3,2,1,0:T(8,128)(2,1)}, u32[]{:S(2)}, u32[]{:S(2)}) collective-permute-start(bf16[4,1,1,64,1536]{4,3,2,1,0:T(8,128)(2,1)} %constant_dynamic-slice_fusion.9), channel_id=1, source_target_pairs={{0,4},{1,5},{2,6},{3,7},{4,0},{5,1},{6,2},{7,3},{8,12},{9,13},{10,... | collective-permute-start | bytes 2359304 | tf_op jit(solution)/shard_map/ppermute | solution.py:38
  331.7 174.8 %collective-permute-start.67 = (bf16[8,144,1024]{2,1,0:T(8,128)(2,1)}, bf16[8,144,1024]{2,1,0:T(8,128)(2,1)}, u32[]{:S(2)}, u32[]{:S(2)}) collective-permute-start(bf16[8,144,1024]{2,1,0:T(8,128)(2,1)} %fusion.4), channel_id=1, source_target_pairs={{0,1},{1,0},{2,3},{3,2},{4,5},{5,4},{6,7},{7,6},{8,9},{9,8},{10,11... | collective-permute-start | bytes 7077896 | tf_op jit(solution)/shard_map/ppermute | solution.py:38
  366.4 23.5 %collective-permute-start.47 = (f32[256,1024]{1,0:T(8,128)}, f32[256,1024]{1,0:T(8,128)S(1)}, u32[]{:S(2)}, u32[]{:S(2)}) collective-permute-start(f32[256,1024]{1,0:T(8,128)} %slice.428), channel_id=1, source_target_pairs={{0,1},{1,0},{2,3},{3,2},{4,5},{5,4},{6,7},{7,6},{8,9},{9,8},{10,11... | collective-permute-start | bytes 3145736 | tf_op jit(solution)/shard_map/ppermute | solution.py:38
  378.3 74.1 %collective-permute-start.56 = (bf16[4,1,2,73,768]{4,0,3,2,1:T(4,128)(2,1)}, bf16[4,1,2,73,768]{4,0,3,2,1:T(4,128)(2,1)}, u32[]{:S(2)}, u32[]{:S(2)}) collective-permute-start(bf16[4,1,2,73,768]{4,0,3,2,1:T(4,128)(2,1)} %copy.117), channel_id=1, source_target_pairs={{0,4},{1,5},{2,6},{3,7},{4,0},{5,1},{6,2},{7,3},{8,12},{9,13},{10,... | collective-permute-start | bytes 2691080 | tf_op jit(solution)/shard_map/ppermute | solution.py:38
  389.9 65.0 %collective-permute-start.54 = (bf16[4,2,1,73,768]{4,0,3,2,1:T(4,128)(2,1)}, bf16[4,2,1,73,768]{4,0,3,2,1:T(4,128)(2,1)}, u32[]{:S(2)}, u32[]{:S(2)}) collective-permute-start(bf16[4,2,1,73,768]{4,0,3,2,1:T(4,128)(2,1)} %copy.115), channel_id=1, source_target_pairs={{0,2},{1,3},{2,0},{3,1},{4,6},{5,7},{6,4},{7,5},{8,10},{9,11},{10,... | collective-permute-start | bytes 2691080 | tf_op jit(solution)/shard_map/ppermute | solution.py:38
  393.4 18.6 %collective-permute-start.49 = (f32[4,2,1,1,64]{4,3,2,1,0:T(1,128)S(1)}, f32[4,2,1,1,64]{4,3,2,1,0:T(1,128)S(1)}, u32[]{:S(2)}, u32[]{:S(2)}) collective-permute-start(f32[4,2,1,1,64]{4,3,2,1,0:T(1,128)S(1)} %constant_dynamic-slice_fusion.26), channel_id=1, source_target_pairs={{0,2},{1,3},{2,0},{3,1},{4,6},{5,7},{6,4},{7,5},{8,10},{9,11},{10,... | collective-permute-start | bytes 6152 | tf_op jit(solution)/shard_map/ppermute | solution.py:38
  412.8 55.3 %collective-permute-start.64 = (bf16[2,1,1,64,3072]{4,3,2,1,0:T(8,128)(2,1)S(1)}, bf16[2,1,1,64,3072]{4,3,2,1,0:T(8,128)(2,1)S(1)}, u32[]{:S(2)}, u32[]{:S(2)}) collective-permute-start(bf16[2,1,1,64,3072]{4,3,2,1,0:T(8,128)(2,1)S(1)} %fusion.12), channel_id=1, source_target_pairs={{0,16},{1,17},{2,18},{3,19},{4,20},{5,21},{6,22},{7,23},{8,24},{9,... | collective-permute-start | bytes 2359304 | tf_op jit(solution)/shard_map/ppermute | solution.py:38
  415.7 33.1 %collective-permute-start.51 = (f32[2,1,1,1,64]{4,3,2,1,0:T(1,128)S(1)}, f32[2,1,1,1,64]{4,3,2,1,0:T(1,128)S(1)}, u32[]{:S(2)}, u32[]{:S(2)}) collective-permute-start(f32[2,1,1,1,64]{4,3,2,1,0:T(1,128)S(1)} %constant_dynamic-slice_fusion.22), channel_id=1, source_target_pairs={{0,16},{1,17},{2,18},{3,19},{4,20},{5,21},{6,22},{7,23},{8,24},{9,... | collective-permute-start | bytes 1544 | tf_op jit(solution)/shard_map/ppermute | solution.py:38
  454.4 10.6 %collective-permute-start.57 = (bf16[4,1,1,73,768]{4,0,3,2,1:T(4,128)(2,1)S(1)}, bf16[4,1,1,73,768]{4,0,3,2,1:T(4,128)(2,1)S(1)}, u32[]{:S(2)}, u32[]{:S(2)}) collective-permute-start(bf16[4,1,1,73,768]{4,0,3,2,1:T(4,128)(2,1)S(1)} %constant_dynamic-slice_fusion.12), channel_id=1, source_target_pairs={{0,2},{1,3},{2,0},{3,1},{4,6},{5,7},{6,4},{7,5},{8,10},{9,11},{10,... | collective-permute-start | bytes 1345544 | tf_op jit(solution)/shard_map/ppermute | solution.py:38
  456.9 10.3 %collective-permute-start.55 = (bf16[4,1,1,73,768]{4,0,3,2,1:T(4,128)(2,1)S(1)}, bf16[4,1,1,73,768]{4,0,3,2,1:T(4,128)(2,1)S(1)}, u32[]{:S(2)}, u32[]{:S(2)}) collective-permute-start(bf16[4,1,1,73,768]{4,0,3,2,1:T(4,128)(2,1)S(1)} %constant_dynamic-slice_fusion.15), channel_id=1, source_target_pairs={{0,4},{1,5},{2,6},{3,7},{4,0},{5,1},{6,2},{7,3},{8,12},{9,13},{10,... | collective-permute-start | bytes 1345544 | tf_op jit(solution)/shard_map/ppermute | solution.py:38
  468.1 19.9 %collective-permute-start.58 = (bf16[2,1,1,73,1536]{4,0,3,2,1:T(2,128)(2,1)S(1)}, bf16[2,1,1,73,1536]{4,0,3,2,1:T(2,128)(2,1)S(1)}, u32[]{:S(2)}, u32[]{:S(2)}) collective-permute-start(bf16[2,1,1,73,1536]{4,0,3,2,1:T(2,128)(2,1)S(1)} %fusion.19), channel_id=1, source_target_pairs={{0,16},{1,17},{2,18},{3,19},{4,20},{5,21},{6,22},{7,23},{8,24},{9,... | collective-permute-start | bytes 1345544 | tf_op jit(solution)/shard_map/ppermute | solution.py:38
  468.4 20.9 %collective-permute-start.65 = (bf16[1,1,1,64,3072]{4,3,2,1,0:T(8,128)(2,1)S(1)}, bf16[1,1,1,64,3072]{4,3,2,1,0:T(8,128)(2,1)S(1)}, u32[]{:S(2)}, u32[]{:S(2)}) collective-permute-start(bf16[1,1,1,64,3072]{4,3,2,1,0:T(8,128)(2,1)S(1)} %constant_dynamic-slice_fusion.6), channel_id=1, source_target_pairs={{0,8},{1,9},{2,10},{3,11},{4,12},{5,13},{6,14},{7,15},{8,0},{9,1},... | collective-permute-start | bytes 1179656 | tf_op jit(solution)/shard_map/ppermute | solution.py:38
  489.2 11.4 %collective-permute-start.59 = (bf16[1,1,1,73,1536]{4,0,3,2,1:T(2,128)(2,1)S(1)}, bf16[1,1,1,73,1536]{4,0,3,2,1:T(2,128)(2,1)S(1)}, u32[]{:S(2)}, u32[]{:S(2)}) collective-permute-start(bf16[1,1,1,73,1536]{4,0,3,2,1:T(2,128)(2,1)S(1)} %constant_dynamic-slice_fusion.11), channel_id=1, source_target_pairs={{0,8},{1,9},{2,10},{3,11},{4,12},{5,13},{6,14},{7,15},{8,0},{9,1},... | collective-permute-start | bytes 672776 | tf_op jit(solution)/shard_map/ppermute | solution.py:38
  504.6 10.1 %collective-permute-start.66 = (f32[32,4608]{1,0:T(8,128)}, f32[32,4608]{1,0:T(8,128)}, u32[]{:S(2)}, u32[]{:S(2)}) collective-permute-start(f32[32,4608]{1,0:T(8,128)} %fusion.16), channel_id=1, source_target_pairs={{0,1},{1,0},{2,3},{3,2},{4,5},{5,4},{6,7},{7,6},{8,9},{9,8},{10,11... | collective-permute-start | bytes 1769480 | tf_op jit(solution)/shard_map/ppermute | solution.py:38
  510.8 28.8 %collective-permute-start.70 = (bf16[4,1,2,144,512]{4,3,2,1,0:T(8,128)(2,1)S(1)}, bf16[4,1,2,144,512]{4,3,2,1,0:T(8,128)(2,1)S(1)}, u32[]{:S(2)}, u32[]{:S(2)}) collective-permute-start(bf16[4,1,2,144,512]{4,3,2,1,0:T(8,128)(2,1)S(1)} %constant_dynamic-slice_fusion.3), channel_id=1, source_target_pairs={{0,4},{1,5},{2,6},{3,7},{4,0},{5,1},{6,2},{7,3},{8,12},{9,13},{10,... | collective-permute-start | bytes 3538952 | tf_op jit(solution)/shard_map/ppermute | solution.py:38
  513.1 28.6 %collective-permute-start.68 = (bf16[4,2,1,144,512]{4,3,2,1,0:T(8,128)(2,1)S(1)}, bf16[4,2,1,144,512]{4,3,2,1,0:T(8,128)(2,1)S(1)}, u32[]{:S(2)}, u32[]{:S(2)}) collective-permute-start(bf16[4,2,1,144,512]{4,3,2,1,0:T(8,128)(2,1)S(1)} %constant_dynamic-slice_fusion.5), channel_id=1, source_target_pairs={{0,2},{1,3},{2,0},{3,1},{4,6},{5,7},{6,4},{7,5},{8,10},{9,11},{10,... | collective-permute-start | bytes 3538952 | tf_op jit(solution)/shard_map/ppermute | solution.py:38
  540.0 15.2 %collective-permute-start.71 = (bf16[4,1,1,144,512]{4,3,2,1,0:T(8,128)(2,1)S(1)}, bf16[4,1,1,144,512]{4,3,2,1,0:T(8,128)(2,1)S(1)}, u32[]{:S(2)}, u32[]{:S(2)}) collective-permute-start(bf16[4,1,1,144,512]{4,3,2,1,0:T(8,128)(2,1)S(1)} %constant_dynamic-slice_fusion.2), channel_id=1, source_target_pairs={{0,2},{1,3},{2,0},{3,1},{4,6},{5,7},{6,4},{7,5},{8,10},{9,11},{10,... | collective-permute-start | bytes 1769480 | tf_op jit(solution)/shard_map/ppermute | solution.py:38
  542.1 14.9 %collective-permute-start.69 = (bf16[4,1,1,144,512]{4,3,2,1,0:T(8,128)(2,1)S(1)}, bf16[4,1,1,144,512]{4,3,2,1,0:T(8,128)(2,1)S(1)}, u32[]{:S(2)}, u32[]{:S(2)}) collective-permute-start(bf16[4,1,1,144,512]{4,3,2,1,0:T(8,128)(2,1)S(1)} %constant_dynamic-slice_fusion.4), channel_id=1, source_target_pairs={{0,4},{1,5},{2,6},{3,7},{4,0},{5,1},{6,2},{7,3},{8,12},{9,13},{10,... | collective-permute-start | bytes 1769480 | tf_op jit(solution)/shard_map/ppermute | solution.py:38
  557.2 27.3 %collective-permute-start.72 = (bf16[2,1,1,144,1024]{4,3,2,1,0:T(8,128)(2,1)S(1)}, bf16[2,1,1,144,1024]{4,3,2,1,0:T(8,128)(2,1)S(1)}, u32[]{:S(2)}, u32[]{:S(2)}) collective-permute-start(bf16[2,1,1,144,1024]{4,3,2,1,0:T(8,128)(2,1)S(1)} %fusion.17), channel_id=1, source_target_pairs={{0,16},{1,17},{2,18},{3,19},{4,20},{5,21},{6,22},{7,23},{8,24},{9,... | collective-permute-start | bytes 1769480 | tf_op jit(solution)/shard_map/ppermute | solution.py:38
  (121 other events, 866.9 us)
